TPU v7x, 512 devices: a whole 4x4x16 slice. The times are simulated.
512 devices in a mesh: prow: 16 (over y, x), pcol: 32 (over z, core).
Axes of the slice: x: 4, y: 4, z: 16, core: 2. Of those that a mesh axis runs over, the one named last changes fastest.
Arguments:
- panel: float32 [65536, 128], P(('prow', 'pcol')), may hold values from -0.0234375 to 0.0234375
- solved: float32 [65536, 8192], P('prow', 'pcol'), may hold values from -6 to 6
- window_rhs: float32 [128, 8192], P('prow', 'pcol'), may hold values from -6 to 6
- coupling: float32 [64, 64], replicated, may hold values from -0.75 to 0.75
- inverses: float32 [2, 64, 64], replicated, may hold values from -0.5 to 1.4, as said below
Outputs:
- window_z: float32 [128, 8192], P('prow', 'pcol')
Inputs may be any that keep to these rules, and one draw needn't show every extreme that they name: `inverses`: each of the two tiles is lower triangular with a positive diagonal.
All inputs are finite; a program needn't handle non-finite values.
Results may differ from a plain program's by a relative error of at most 0.00007.
Values sent between devices are 32-bit elements; how exact they have to be, the bound alone decides.
No kernel may reach another device: no remote copies, remote signals or barrier semaphores. Data moves between devices by JAX's collectives and lax.ppermute only.
A program may use at most 64 MiB of HBM per device.

v0:
```python
import jax
import jax.numpy as jnp
from jax import lax
from jax.sharding import PartitionSpec as P


def transposed_product(left, right):
    return lax.dot_general(
        left,
        right,
        (((0,), (0,)), ((), ())),
        precision=lax.Precision.HIGHEST,
        preferred_element_type=jnp.float32,
    )


def body(panel, solved, window_rhs, coupling, inverses):
    block_rows = coupling.shape[0]
    share_rows = window_rhs.shape[0]
    row_index = lax.axis_index("prow")
    update = transposed_product(lax.all_gather(panel, "pcol", axis=0, tiled=True), solved)
    own_start = row_index * share_rows
    negated = -update
    own_part = lax.dynamic_slice_in_dim(negated, own_start, share_rows, 0) + window_rhs
    negated = lax.dynamic_update_slice_in_dim(negated, own_part, own_start, 0)
    remainder = lax.psum(negated, "prow")
    later_block = transposed_product(inverses[1], remainder[block_rows:])
    carried = remainder[:block_rows] - transposed_product(coupling, later_block)
    first_block = transposed_product(inverses[0], carried)
    window_z = jnp.concatenate([first_block, later_block], axis=0)
    return lax.dynamic_slice_in_dim(window_z, row_index * share_rows, share_rows, 0)


def solution(mesh):
    placed = (P(("prow", "pcol"), None), P("prow", "pcol"), P("prow", "pcol"), P(), P())
    return jax.shard_map(
        body, mesh=mesh, in_specs=placed, out_specs=P("prow", "pcol"), check_vma=False
    )
```

profile of v0, /device:TPU:1, one launch (start us, length us, event | category | flops | bytes accessed | tf_op | source)
XLA Modules:
  0.0 212.1 jit_solution(222117463060469708)
XLA Ops:
  6.5 0.0 copy-start
  6.5 0.0 copy-start.3
  6.5 0.0 copy-start.2
  6.5 0.0 all-gather.2.cloned.1.call-start
  6.5 0.7 all-gather.2.cloned.1.call-update
  7.3 0.0 all-reduce.2.cloned.1.call-start
  7.3 79.7 %all-gather.2.cloned.1.call-done = f32[4096,128]{1,0:T(8,128)} async-done(((f32[128,128]{1,0:T(8,128)}), f32[4096,128]{1,0:T(8,128)}) %all-gather.2.cloned.1.call-update) | async-done | bytes 2097168 | tf_op jit(solution)/shard_map/all_gather | solution.py:21
  87.0 6.3 %convolution_negate_fusion = f32[128,256]{1,0:T(8,128)S(1)} fusion(f32[4096,128]{1,0:T(8,128)} %all-gather.2.cloned.1.call-done, f32[4096,256]{1,0:T(8,128)} %param.6), kind=kOutput, calls=%fused_computation | convolution fusion | flops 1610645504 | bytes 6422528 | tf_op jit(solution)/shard_map/dot_general | solution.py:8
  93.4 0.0 copy-done.3
  93.4 0.0 copy-start.1
  93.4 0.6 copy-done.1
  94.1 0.0 all-reduce.2.cloned.1.call-update
  94.1 108.1 %all-reduce.2.cloned.1.call-done = f32[128,256]{1,0:T(8,128)} async-done(((f32[128,256]{1,0:T(8,128)}), f32[128,256]{1,0:T(8,128)}) %all-reduce.2.cloned.1.call-update) | async-done | bytes 131088 | tf_op jit(solution)/shard_map/psum | solution.py:26
  202.2 0.0 copy-done.2
  202.2 1.1 fusion.1
  203.3 0.0 copy-done
  203.3 1.1 fusion
  204.4 0.3 convolution_bitcast_fusion
  204.6 0.6 fusion.7
  (1 shorter events, 0.0 us)
Async XLA Ops:
  6.5 196.7 %copy-start = (f32[64,64]{1,0:T(8,128)S(1)}, f32[64,64]{1,0:T(8,128)}, u32[]{:S(2)}) copy-start(f32[64,64]{1,0:T(8,128)} %param.8) | copy-start | bytes 49156
  6.5 86.8 %copy-start.3 = (f32[8,256]{1,0:T(8,128)S(1)}, f32[8,256]{1,0:T(8,128)}, u32[]{:S(2)}) copy-start(f32[8,256]{1,0:T(8,128)} %param.7) | copy-start | bytes 24580
  6.5 195.6 %copy-start.2 = (f32[2,64,64]{2,1,0:T(8,128)S(1)}, f32[2,64,64]{2,1,0:T(8,128)}, u32[]{:S(2)}) copy-start(f32[2,64,64]{2,1,0:T(8,128)} %param.9) | copy-start | bytes 98308
  6.5 80.5 %all-gather.2.cloned.1.call-start = ((), (), s32[]{:S(2)}) async-start(), calls=%async_computation | async-start | bytes 2162688 | tf_op jit(solution)/shard_map/all_gather | solution.py:21
  7.3 194.9 %all-reduce.2.cloned.1.call-start = ((), (), s32[]{:S(2)}) async-start(), calls=%async_computation.1 | async-start | bytes 262144 | tf_op jit(solution)/shard_map/psum | solution.py:26
  93.4 0.7 copy-start.1
Sparse Core Ops, SparseCore 0:
  9.5 77.5 all-gather.1
  94.2 107.9 all-reduce.1
where the time goes:
time: 213 us; the launch traced here: 212 us
  waiting for transfers between devices  189 us (89%)
  between operations  13.5 us (6%)
  matrix products  8.77 us (4%)
    psum x1, waiting for transfers between devices, body(): remainder = lax.psum(negated, 'prow')  108 us
    all_gather x1, waiting for transfers between devices, body(): lax.all_gather(panel, 'pcol', axis=0, tiled=True)  79.7 us
    dot_general x4, matrix products, transposed_product(): lax.dot_general(left, right, (((0,), (0,)), ((), ())), precision=lax.Prec...  8.77 us
  transfers between devices with their start and end apart: 2, of which 2 were waited for; matrix products, arithmetic and copies ran while one was open for 0% of the time, Pallas kernels for 0%

commit v1 on v0

v1 whole, which is shorter than its diff:
```python
import jax
import jax.numpy as jnp
from jax import lax
from jax.sharding import PartitionSpec as P

GATHERED = 120


def transposed_product(left, right, precision=lax.Precision.HIGHEST):
    return lax.dot_general(
        left,
        right,
        (((0,), (0,)), ((), ())),
        precision=precision,
        preferred_element_type=jnp.float32,
    )


def body(panel, solved, window_rhs, coupling, inverses):
    block_rows = coupling.shape[0]
    share_rows = window_rhs.shape[0]
    panel_rows, panel_columns = panel.shape
    columns = window_rhs.shape[1]
    grid_rows = lax.axis_size("prow")
    grid_columns = lax.axis_size("pcol")
    chips = grid_columns // 2
    row_index = lax.axis_index("prow")
    core = lax.axis_index("pcol") % 2
    same_core = [[2 * z + c for z in range(chips)] for c in range(2)]
    rest = jnp.broadcast_to(panel[None, GATHERED:], (chips, panel_rows - GATHERED, panel_columns))
    rest = lax.all_to_all(rest, "pcol", 0, 0, axis_index_groups=same_core)
    most = lax.all_gather(panel[:GATHERED], "pcol", axis=0, axis_index_groups=same_core)
    own = jnp.concatenate([most, rest], axis=1).reshape(chips * panel_rows, panel_columns)
    other = lax.ppermute(own, "pcol", [(i, i ^ 1) for i in range(grid_columns)])
    tiles = solved.reshape(chips, 2, panel_rows, columns)
    own_rows = lax.dynamic_index_in_dim(tiles, core, 1, False).reshape(-1, columns)
    other_rows = lax.dynamic_index_in_dim(tiles, 1 - core, 1, False).reshape(-1, columns)
    update = transposed_product(own, own_rows, lax.Precision.HIGH)
    update = update + transposed_product(other, other_rows, lax.Precision.HIGH)
    negated = -update
    own_start = row_index * share_rows
    own_part = lax.dynamic_slice_in_dim(negated, own_start, share_rows, 0) + window_rhs
    remainder = lax.dynamic_update_slice_in_dim(negated, own_part, own_start, 0)
    later_block = transposed_product(inverses[1], remainder[block_rows:])
    carried = remainder[:block_rows] - transposed_product(coupling, later_block)
    first_block = transposed_product(inverses[0], carried)
    window_z = jnp.concatenate([first_block, later_block], axis=0)
    parts = window_z.reshape(grid_rows, share_rows, columns)
    return jnp.sum(lax.all_to_all(parts, "prow", 0, 0), axis=0)


def solution(mesh):
    placed = (P(("prow", "pcol"), None), P("prow", "pcol"), P("prow", "pcol"), P(), P())
    return jax.shard_map(
        body, mesh=mesh, in_specs=placed, out_specs=P("prow", "pcol"), check_vma=False
    )
```

time: 213 us -> 76.8 us (0.36)
  waiting for transfers between devices: 189 us -> 0.01 us
  blocking collectives: 0 us -> 43 us
  starting transfers between devices: 0.04 us -> 25 us
  between operations: 13.5 us -> 0.16 us
  matrix products: 8.77 us -> 2.78 us
  local copies, waits for them, and re-layouts: 0.66 us -> 4.76 us
    psum x1 -> x0, waiting for transfers between devices: 108 us -> none  [body(): remainder = lax.psum(negated, 'prow')]
    all_gather x1 -> x0, waiting for transfers between devices: 79.7 us -> none  [body(): lax.all_gather(panel, 'pcol', axis=0, tiled=True)]
    all_gather x0 -> x1, blocking collectives: none -> 29.3 us  [body(): lax.all_gather(panel[:GATHERED], 'pcol', axis=0, axis_index_groups=same_c...]
    all_to_all x0 -> x1, starting transfers between devices: none -> 15.7 us  [body(): rest = lax.all_to_all(rest, 'pcol', 0, 0, axis_index_groups=same_core)]
    all_to_all x0 -> x1, blocking collectives: none -> 13.7 us  [body(): return jnp.sum(lax.all_to_all(parts, 'prow', 0, 0), axis=0)]
    ppermute x0 -> x1, starting transfers between devices: none -> 9.25 us  [body(): other = lax.ppermute(own, 'pcol', [(i, i ^ 1) for i in range(grid_columns)])]
    dot_general x4 -> x5, matrix products: 8.77 us -> 2.78 us  [transposed_product(): lax.dot_general(left, right, (((0,), (0,)), ((), ())), precision=precisio...]
    dynamic_slice x0 -> x1, local copies, waits for them, and re-layouts: none -> 2.59 us  [body(): lax.dynamic_index_in_dim(tiles, 1 - core, 1, False).reshape(-1, columns)]
  transfers between devices with their start and end apart: 2 -> 2, of which waited for: 2 -> 0; matrix products, arithmetic and copies ran while one was open for 0% -> 6% of each run, Pallas kernels for 0% -> 0%
where the time goes in v1:
time: 76.8 us; the launch traced here: 76.5 us
  blocking collectives  43 us (56%)
  starting transfers between devices  25 us (33%)
  local copies, waits for them, and re-layouts  4.76 us (6%)
  matrix products  2.78 us (4%)
    all_gather x1, blocking collectives, body(): lax.all_gather(panel[:GATHERED], 'pcol', axis=0, axis_index_groups=same_c...  29.3 us
    all_to_all x1, starting transfers between devices, body(): rest = lax.all_to_all(rest, 'pcol', 0, 0, axis_index_groups=same_core)  15.7 us
    all_to_all x1, blocking collectives, body(): return jnp.sum(lax.all_to_all(parts, 'prow', 0, 0), axis=0)  13.7 us
    ppermute x1, starting transfers between devices, body(): other = lax.ppermute(own, 'pcol', [(i, i ^ 1) for i in range(grid_columns)])  9.25 us
    dot_general x5, matrix products, transposed_product(): lax.dot_general(left, right, (((0,), (0,)), ((), ())), precision=precisio...  2.78 us
    dynamic_slice x1, local copies, waits for them, and re-layouts, body(): lax.dynamic_index_in_dim(tiles, 1 - core, 1, False).reshape(-1, columns)  2.59 us
  transfers between devices with their start and end apart: 2, of which 0 were waited for; matrix products, arithmetic and copies ran while one was open for 6% of the time, Pallas kernels for 0%

profile of v1, /device:TPU:1, one launch (start us, length us, event | category | flops | bytes accessed | tf_op | source)
XLA Modules:
  0.0 76.5 jit_solution(14918369339834992123)
XLA Ops:
  0.0 0.0 copy-start
  0.0 0.7 slice.19
  0.7 0.6 broadcast_in_dim.2
  1.3 15.7 %all-to-all-start = ((f32[16,8,128]{2,1,0:T(8,128)}), f32[16,8,128]{2,1,0:T(8,128)S(1)}, u32[]{:S(2)}, u32[]{:S(2)}) async-start(f32[16,8,128]{2,1,0:T(8,128)} %broadcast_in_dim.2), calls=%async_computation | async-start | bytes 131072 | tf_op jit(solution)/shard_map/all_to_all | solution.py:31
  17.1 0.8 %slice.18 = f32[120,128]{1,0:T(8,128)S(1)} slice(f32[128,128]{1,0:T(8,128)} %param.5), slice={[0:120], [0:128]} | slice | bytes 122880 | tf_op jit(solution)/shard_map/slice | solution.py:32
  17.9 29.3 %all-gather = f32[1920,128]{1,0:T(8,128)S(1)} all-gather(f32[120,128]{1,0:T(8,128)S(1)} %slice.18), channel_id=2, replica_groups={{0,2,4,6,8,10,12,14,16,18,20,22,24,26,28,30},{1,3,5,7,9,11,13,15,17,19,..., dimensions={0}, use_global_device_ids=true | all-gather | bytes 1044480 | tf_op jit(solution)/shard_map/all_gather | solution.py:32
  47.2 0.0 all-to-all-done
  47.3 0.1 pad_maximum_fusion
  47.4 9.3 %collective-permute-start = (f32[2048,128]{1,0:T(8,128)S(1)}, f32[2048,128]{1,0:T(8,128)S(1)}, u32[]{:S(2)}, u32[]{:S(2)}) collective-permute-start(f32[2048,128]{1,0:T(8,128)S(1)} %bitcast.26), channel_id=1, source_target_pairs={{0,1},{1,0},{2,3},{3,2},{4,5},{5,4},{6,7},{7,6},{8,9},{9,8},{10,11... | collective-permute-start | bytes 3145736 | tf_op jit(solution)/shard_map/ppermute | solution.py:34
  56.6 2.6 %constant_dynamic-slice_fusion = (f32[16,1,128,256]{3,2,1,0:T(8,128)S(1)}, f32[16,1,128,256]{3,2,1,0:T(8,128)S(1)}) fusion(f32[16,2,128,256]{3,2,1,0:T(8,128)} %bitcast.28, s32[]{:T(128)S(6)} %select_n.20, s32[]{:T(128)S(6)} %select_n.19), kind=kLoop, calls=%fused_computation.14 | loop fusion | bytes 8388616 | tf_op jit(solution)/shard_map/jit(dynamic_index_in_dim)/dynamic_slice | solution.py:37
  59.2 1.0 %fusion.7 = f32[128,256]{1,0:T(8,128)S(1)} fusion(f32[2048,128]{1,0:T(8,128)S(1)} %bitcast.27, f32[2048,256]{1,0:T(8,128)S(1)} %bitcast.24), kind=kOutput, calls=%fused_computation.16 | convolution fusion | flops 402653184 | bytes 3276800 | tf_op jit(solution)/shard_map/dot_general | solution.py:10
  60.3 0.0 copy-start.2
  60.3 0.0 copy-start.1
  60.3 0.0 collective-permute-done
  60.3 1.0 %fusion = f32[128,256]{1,0:T(8,128)S(1)} fusion(f32[128,256]{1,0:T(8,128)S(1)} %fusion.7, f32[2048,128]{1,0:T(8,128)S(1)} %collective-permute-done, f32[2048,256]{1,0:T(8,128)S(1)} %bitcast.25), kind=kOutput, calls=%fused_computation.1 | convolution fusion | flops 402718720 | bytes 3407872 | tf_op jit(solution)/shard_map/dot_general | solution.py:10
  61.3 0.0 copy-done.2
  61.3 0.0 copy-done.1
  61.3 0.3 fusion.1
  61.6 0.0 copy-done
  61.6 0.3 convolution_bitcast_fusion.1
  61.9 0.3 convolution_bitcast_fusion
  62.2 13.7 %all_to_all.10 = f32[16,8,256]{2,1,0:T(8,128)S(1)} all-to-all(f32[16,8,256]{2,1,0:T(8,128)S(1)} %maximum_bitcast_fusion), channel_id=1, replica_groups=mesh['prow'=16,'pcol'=32] {'prow'}, dimensions={0} | all-to-all | bytes 262144 | tf_op jit(solution)/shard_map/all_to_all | solution.py:49
  75.9 0.6 reduce_sum.9
  (2 shorter events, 0.0 us)
Async XLA Ops:
  0.0 61.6 %copy-start = (f32[64,64]{1,0:T(8,128)S(1)}, f32[64,64]{1,0:T(8,128)}, u32[]{:S(2)}) copy-start(f32[64,64]{1,0:T(8,128)} %param.8) | copy-start | bytes 49156
  1.3 45.9 %all-to-all-start = ((f32[16,8,128]{2,1,0:T(8,128)}), f32[16,8,128]{2,1,0:T(8,128)S(1)}, u32[]{:S(2)}, u32[]{:S(2)}) async-start(f32[16,8,128]{2,1,0:T(8,128)} %broadcast_in_dim.2), calls=%async_computation | async-start | bytes 131072 | tf_op jit(solution)/shard_map/all_to_all | solution.py:31
  47.4 12.9 %collective-permute-start = (f32[2048,128]{1,0:T(8,128)S(1)}, f32[2048,128]{1,0:T(8,128)S(1)}, u32[]{:S(2)}, u32[]{:S(2)}) collective-permute-start(f32[2048,128]{1,0:T(8,128)S(1)} %bitcast.26), channel_id=1, source_target_pairs={{0,1},{1,0},{2,3},{3,2},{4,5},{5,4},{6,7},{7,6},{8,9},{9,8},{10,11... | collective-permute-start | bytes 3145736 | tf_op jit(solution)/shard_map/ppermute | solution.py:34
  60.3 1.1 %copy-start.2 = (f32[8,256]{1,0:T(8,128)S(1)}, f32[8,256]{1,0:T(8,128)}, u32[]{:S(2)}) copy-start(f32[8,256]{1,0:T(8,128)} %param.7) | copy-start | bytes 24580
  60.3 1.1 %copy-start.1 = (f32[2,64,64]{2,1,0:T(8,128)S(1)}, f32[2,64,64]{2,1,0:T(8,128)}, u32[]{:S(2)}) copy-start(f32[2,64,64]{2,1,0:T(8,128)} %param.9) | copy-start | bytes 98308

commit v2 on v1

v2 whole, which is shorter than its diff:
```python
import jax
import jax.numpy as jnp
from jax import lax
from jax.sharding import PartitionSpec as P

STRIDE = 4


def transposed_product(left, right, precision=lax.Precision.HIGHEST):
    return lax.dot_general(
        left,
        right,
        (((0,), (0,)), ((), ())),
        precision=precision,
        preferred_element_type=jnp.float32,
    )


def body(panel, solved, window_rhs, coupling, inverses):
    block_rows = coupling.shape[0]
    share_rows, columns = window_rhs.shape
    panel_rows, panel_columns = panel.shape
    grid_rows = lax.axis_size("prow")
    grid_columns = lax.axis_size("pcol")
    chips = grid_columns // 2
    far = chips // STRIDE
    row_index = lax.axis_index("prow")
    column_index = lax.axis_index("pcol")
    core = column_index % 2
    place = (column_index // 2) % STRIDE

    def shifted(array, up, down):
        pairs = [(2 * z + c, 2 * ((z + (up, down)[c]) % chips) + c) for z in range(chips) for c in range(2)]
        return lax.ppermute(array, "pcol", pairs)

    def swapped(array):
        return lax.ppermute(array, "pcol", [(i, i ^ 1) for i in range(grid_columns)])

    groups = [[2 * (STRIDE * h + l) + c for h in range(far)] for l in range(STRIDE) for c in range(2)]
    own = lax.all_gather(panel, "pcol", axis=0, axis_index_groups=groups, tiled=True)
    bundles = [own, shifted(own, 1, 1), shifted(own, -1, -1), shifted(own, 2, -2)]
    offsets = [0, -1, 1, 2]
    tiles = solved.reshape(far, STRIDE, 2, panel_rows, columns)

    def rows_of(offset, which):
        start = (0, (place + offset) % STRIDE, which, 0, 0)
        part = lax.dynamic_slice(tiles, start, (far, 1, 1, panel_rows, columns))
        return part.reshape(far * panel_rows, columns)

    update = 0.0
    for bundle, offset in zip(bundles, offsets):
        update += transposed_product(bundle, rows_of(offset, core), lax.Precision.HIGH)
        update += transposed_product(swapped(bundle), rows_of(offset, 1 - core), lax.Precision.HIGH)
    negated = -update
    own_start = row_index * share_rows
    own_part = lax.dynamic_slice_in_dim(negated, own_start, share_rows, 0) + window_rhs
    remainder = lax.dynamic_update_slice_in_dim(negated, own_part, own_start, 0)
    later_block = transposed_product(inverses[1], remainder[block_rows:])
    carried = remainder[:block_rows] - transposed_product(coupling, later_block)
    first_block = transposed_product(inverses[0], carried)
    window_z = jnp.concatenate([first_block, later_block], axis=0)
    parts = window_z.reshape(grid_rows, share_rows, columns)
    return jnp.sum(lax.all_to_all(parts, "prow", 0, 0), axis=0)


def solution(mesh):
    placed = (P(("prow", "pcol"), None), P("prow", "pcol"), P("prow", "pcol"), P(), P())
    return jax.shard_map(
        body, mesh=mesh, in_specs=placed, out_specs=P("prow", "pcol"), check_vma=False
    )
```

time: 76.8 us -> 75.2 us (0.979)
  matrix products: 2.78 us -> 7.99 us
  blocking collectives: 43 us -> 39.3 us
  starting transfers between devices: 25 us -> 22.2 us
  local copies, waits for them, and re-layouts: 4.76 us -> 3.54 us
    all_to_all x1 -> x0, starting transfers between devices: 15.7 us -> none  [body(): rest = lax.all_to_all(rest, 'pcol', 0, 0, axis_index_groups=same_core)]
    ppermute x1 -> x7, starting transfers between devices: 9.25 us -> 22.2 us  [the longest x4 13.5 us: swapped(): lax.ppermute(array, 'pcol', [(i, i ^ 1) for i in range(grid_columns)])]
    dot_general x5 -> x11, matrix products: 2.78 us -> 7.99 us  [transposed_product(): lax.dot_general(left, right, (((0,), (0,)), ((), ())), precision=precisio...]
    all_gather x1, blocking collectives: 29.3 us -> 25.6 us  [body(): lax.all_gather(panel, 'pcol', axis=0, axis_index_groups=groups, tiled=True)]
    slice x2 -> x0, local copies, waits for them, and re-layouts: 1.53 us -> none  [the longest x1 0.84 us: body(): panel[:GATHERED]]
    dynamic_slice x1, local copies, waits for them, and re-layouts: 2.59 us -> 3.51 us  [rows_of(): part = lax.dynamic_slice(tiles, start, (far, 1, 1, panel_rows, columns))]
  transfers between devices with their start and end apart: 2 -> 7, of which waited for: 0 -> 1; matrix products, arithmetic and copies ran while one was open for 6% -> 14% of each run, Pallas kernels for 0% -> 0%
where the time goes in v2:
time: 75.2 us; the launch traced here: 74.7 us
  blocking collectives  39.3 us (52%)
  starting transfers between devices  22.2 us (30%)
  matrix products  7.99 us (11%)
  local copies, waits for them, and re-layouts  3.54 us (5%)
    all_gather x1, blocking collectives, body(): lax.all_gather(panel, 'pcol', axis=0, axis_index_groups=groups, tiled=True)  25.6 us
    all_to_all x1, blocking collectives, body(): return jnp.sum(lax.all_to_all(parts, 'prow', 0, 0), axis=0)  13.7 us
    ppermute x4, starting transfers between devices, swapped(): lax.ppermute(array, 'pcol', [(i, i ^ 1) for i in range(grid_columns)])  13.5 us
    ppermute x3, starting transfers between devices, shifted(): return lax.ppermute(array, 'pcol', pairs)  8.7 us
    dot_general x11, matrix products, transposed_product(): lax.dot_general(left, right, (((0,), (0,)), ((), ())), precision=precisio...  7.99 us
    dynamic_slice x1, local copies, waits for them, and re-layouts, rows_of(): part = lax.dynamic_slice(tiles, start, (far, 1, 1, panel_rows, columns))  3.51 us
  transfers between devices with their start and end apart: 7, of which 1 were waited for; matrix products, arithmetic and copies ran while one was open for 14% of the time, Pallas kernels for 0%

profile of v2, /device:TPU:1, one launch (start us, length us, event | category | flops | bytes accessed | tf_op | source)
XLA Modules:
  0.0 74.7 jit_solution(12485641337738745418)
XLA Ops:
  0.0 0.0 copy-start
  0.0 25.6 %all_gather.3 = f32[512,128]{1,0:T(8,128)S(1)} all-gather(f32[128,128]{1,0:T(8,128)} %param.5), channel_id=1, replica_groups={{0,8,16,24},{1,9,17,25},{2,10,18,26},{3,11,19,27},{4,12,20,28},{5,13,21..., dimensions={0}, use_global_device_ids=true | all-gather | bytes 327680 | tf_op jit(solution)/shard_map/all_gather | solution.py:40
  25.6 5.0 %collective-permute-start = (f32[512,128]{1,0:T(8,128)S(1)}, f32[512,128]{1,0:T(8,128)}, u32[]{:S(2)}, u32[]{:S(2)}) collective-permute-start(f32[512,128]{1,0:T(8,128)S(1)} %all_gather.3), channel_id=1, source_target_pairs={{0,1},{1,0},{2,3},{3,2},{4,5},{5,4},{6,7},{7,6},{8,9},{9,8},{10,11... | collective-permute-start | bytes 786440 | tf_op jit(solution)/shard_map/ppermute | solution.py:37
  30.6 2.6 %collective-permute-start.1 = (f32[512,128]{1,0:T(8,128)S(1)}, f32[512,128]{1,0:T(8,128)}, u32[]{:S(2)}, u32[]{:S(2)}) collective-permute-start(f32[512,128]{1,0:T(8,128)S(1)} %all_gather.3), channel_id=1, source_target_pairs={{0,2},{1,3},{2,4},{3,5},{4,6},{5,7},{6,8},{7,9},{8,10},{9,11},{10,... | collective-permute-start | bytes 786440 | tf_op jit(solution)/shard_map/ppermute | solution.py:34
  33.3 3.9 %collective-permute-start.3 = (f32[512,128]{1,0:T(8,128)S(1)}, f32[512,128]{1,0:T(8,128)}, u32[]{:S(2)}, u32[]{:S(2)}) collective-permute-start(f32[512,128]{1,0:T(8,128)S(1)} %all_gather.3), channel_id=1, source_target_pairs={{0,30},{1,31},{2,0},{3,1},{4,2},{5,3},{6,4},{7,5},{8,6},{9,7},{10,... | collective-permute-start | bytes 786440 | tf_op jit(solution)/shard_map/ppermute | solution.py:34
  37.2 2.2 %collective-permute-start.5 = (f32[512,128]{1,0:T(8,128)S(1)}, f32[512,128]{1,0:T(8,128)}, u32[]{:S(2)}, u32[]{:S(2)}) collective-permute-start(f32[512,128]{1,0:T(8,128)S(1)} %all_gather.3), channel_id=1, source_target_pairs={{0,4},{1,29},{2,6},{3,31},{4,8},{5,1},{6,10},{7,3},{8,12},{9,5},{1... | collective-permute-start | bytes 786440 | tf_op jit(solution)/shard_map/ppermute | solution.py:34
  39.5 3.5 %constant_dynamic-slice_fusion = (f32[4,1,1,128,256]{4,3,2,1,0:T(8,128)S(1)}, f32[4,1,1,128,256]{4,3,2,1,0:T(8,128)S(1)}, f32[4,1,1,128,256]{4,3,2,1,0:T(8,128)S...) fusion(f32[4,4,2,128,256]{4,3,2,1,0:T(8,128)} %bitcast.45, ...), kind=kLoop, calls=%fused_computation.20 | loop fusion | bytes 8388632 | tf_op jit(solution)/shard_map/dynamic_slice | solution.py:47
  43.0 0.4 fusion.10
  43.4 0.0 collective-permute-done.1
  43.4 2.3 %collective-permute-start.2 = (f32[512,128]{1,0:T(8,128)}, f32[512,128]{1,0:T(8,128)S(1)}, u32[]{:S(2)}, u32[]{:S(2)}) collective-permute-start(f32[512,128]{1,0:T(8,128)} %collective-permute-done.1), channel_id=1, source_target_pairs={{0,1},{1,0},{2,3},{3,2},{4,5},{5,4},{6,7},{7,6},{8,9},{9,8},{10,11... | collective-permute-start | bytes 786440 | tf_op jit(solution)/shard_map/ppermute | solution.py:37
  45.8 0.0 collective-permute-done.3
  45.8 3.2 %collective-permute-start.4 = (f32[512,128]{1,0:T(8,128)}, f32[512,128]{1,0:T(8,128)S(1)}, u32[]{:S(2)}, u32[]{:S(2)}) collective-permute-start(f32[512,128]{1,0:T(8,128)} %collective-permute-done.3), channel_id=1, source_target_pairs={{0,1},{1,0},{2,3},{3,2},{4,5},{5,4},{6,7},{7,6},{8,9},{9,8},{10,11... | collective-permute-start | bytes 786440 | tf_op jit(solution)/shard_map/ppermute | solution.py:37
  48.9 0.7 collective-permute-done.5
  49.6 3.0 %collective-permute-start.6 = (f32[512,128]{1,0:T(8,128)}, f32[512,128]{1,0:T(8,128)S(1)}, u32[]{:S(2)}, u32[]{:S(2)}) collective-permute-start(f32[512,128]{1,0:T(8,128)} %collective-permute-done.5), channel_id=1, source_target_pairs={{0,1},{1,0},{2,3},{3,2},{4,5},{5,4},{6,7},{7,6},{8,9},{9,8},{10,11... | collective-permute-start | bytes 786440 | tf_op jit(solution)/shard_map/ppermute | solution.py:37
  52.6 0.0 collective-permute-done
  52.6 1.5 %convolution_add_fusion.4 = f32[256,128]{0,1:T(8,128)S(1)} fusion(f32[256,128]{0,1:T(8,128)S(1)} %fusion.10, f32[512,256]{1,0:T(8,128)} %bitcast.53, f32[512,128]{1,0:T(8,128)} %collective-permute-done), kind=kOutput, calls=%fused_computation.7 | convolution fusion | flops 100696064 | bytes 1048576 | tf_op jit(solution)/shard_map/dot_general | solution.py:10
  54.1 1.5 %convolution_add_fusion.3 = f32[256,128]{0,1:T(8,128)S(1)} fusion(f32[256,128]{0,1:T(8,128)S(1)} %convolution_add_fusion.4, f32[512,256]{1,0:T(8,128)} %bitcast.52, f32[512,128]{1,0:T(8,128)} %collective-permute-done.1), kind=kOutput, calls=%fused_computation.6 | convolution fusion | flops 100696064 | bytes 1048576 | tf_op jit(solution)/shard_map/dot_general | solution.py:10
  55.6 1.3 %fusion.11 = f32[256,128]{0,1:T(8,128)S(1)} fusion(f32[512,256]{1,0:T(8,128)S(1)} %bitcast.47, f32[512,128]{1,0:T(8,128)} %collective-permute-done.3), kind=kOutput, calls=%fused_computation.29 | convolution fusion | flops 100663296 | bytes 917504 | tf_op jit(solution)/shard_map/dot_general | solution.py:10
  56.9 1.3 %fusion.12 = f32[256,128]{0,1:T(8,128)S(1)} fusion(f32[512,256]{1,0:T(8,128)S(1)} %bitcast.46, f32[512,128]{1,0:T(8,128)} %collective-permute-done.5), kind=kOutput, calls=%fused_computation.30 | convolution fusion | flops 100663296 | bytes 917504 | tf_op jit(solution)/shard_map/dot_general | solution.py:10
  58.3 0.0 collective-permute-done.2
  58.3 0.4 fusion.2
  58.7 0.0 collective-permute-done.4
  58.7 0.4 fusion.1
  59.1 0.0 collective-permute-done.6
  59.1 0.4 fusion
  59.5 0.0 copy-done.2
  59.6 0.0 copy-done.1
  59.6 0.3 fusion.3
  59.8 0.3 convolution_bitcast_fusion.1
  60.1 0.3 convolution_bitcast_fusion
  60.4 13.7 %all_to_all.5 = f32[16,8,256]{2,1,0:T(8,128)S(1)} all-to-all(f32[16,8,256]{2,1,0:T(8,128)S(1)} %maximum_bitcast_fusion), channel_id=1, replica_groups=mesh['prow'=16,'pcol'=32] {'prow'}, dimensions={0} | all-to-all | bytes 262144 | tf_op jit(solution)/shard_map/all_to_all | solution.py:63
  74.1 0.6 reduce_sum.9
  (6 shorter events, 0.0 us)
Async XLA Ops:
  0.0 59.8 %copy-start = (f32[64,64]{1,0:T(8,128)S(1)}, f32[64,64]{1,0:T(8,128)}, u32[]{:S(2)}) copy-start(f32[64,64]{1,0:T(8,128)} %param.8) | copy-start | bytes 49156
  25.6 27.0 %collective-permute-start = (f32[512,128]{1,0:T(8,128)S(1)}, f32[512,128]{1,0:T(8,128)}, u32[]{:S(2)}, u32[]{:S(2)}) collective-permute-start(f32[512,128]{1,0:T(8,128)S(1)} %all_gather.3), channel_id=1, source_target_pairs={{0,1},{1,0},{2,3},{3,2},{4,5},{5,4},{6,7},{7,6},{8,9},{9,8},{10,11... | collective-permute-start | bytes 786440 | tf_op jit(solution)/shard_map/ppermute | solution.py:37
  30.6 12.8 %collective-permute-start.1 = (f32[512,128]{1,0:T(8,128)S(1)}, f32[512,128]{1,0:T(8,128)}, u32[]{:S(2)}, u32[]{:S(2)}) collective-permute-start(f32[512,128]{1,0:T(8,128)S(1)} %all_gather.3), channel_id=1, source_target_pairs={{0,2},{1,3},{2,4},{3,5},{4,6},{5,7},{6,8},{7,9},{8,10},{9,11},{10,... | collective-permute-start | bytes 786440 | tf_op jit(solution)/shard_map/ppermute | solution.py:34
  33.3 12.5 %collective-permute-start.3 = (f32[512,128]{1,0:T(8,128)S(1)}, f32[512,128]{1,0:T(8,128)}, u32[]{:S(2)}, u32[]{:S(2)}) collective-permute-start(f32[512,128]{1,0:T(8,128)S(1)} %all_gather.3), channel_id=1, source_target_pairs={{0,30},{1,31},{2,0},{3,1},{4,2},{5,3},{6,4},{7,5},{8,6},{9,7},{10,... | collective-permute-start | bytes 786440 | tf_op jit(solution)/shard_map/ppermute | solution.py:34
  37.2 12.4 %collective-permute-start.5 = (f32[512,128]{1,0:T(8,128)S(1)}, f32[512,128]{1,0:T(8,128)}, u32[]{:S(2)}, u32[]{:S(2)}) collective-permute-start(f32[512,128]{1,0:T(8,128)S(1)} %all_gather.3), channel_id=1, source_target_pairs={{0,4},{1,29},{2,6},{3,31},{4,8},{5,1},{6,10},{7,3},{8,12},{9,5},{1... | collective-permute-start | bytes 786440 | tf_op jit(solution)/shard_map/ppermute | solution.py:34
  43.0 16.5 %copy-start.2 = (f32[8,256]{1,0:T(8,128)S(1)}, f32[8,256]{1,0:T(8,128)}, u32[]{:S(2)}) copy-start(f32[8,256]{1,0:T(8,128)} %param.7) | copy-start | bytes 24580
  43.0 16.6 %copy-start.1 = (f32[2,64,64]{2,1,0:T(8,128)S(1)}, f32[2,64,64]{2,1,0:T(8,128)}, u32[]{:S(2)}) copy-start(f32[2,64,64]{2,1,0:T(8,128)} %param.9) | copy-start | bytes 98308
  43.4 14.9 %collective-permute-start.2 = (f32[512,128]{1,0:T(8,128)}, f32[512,128]{1,0:T(8,128)S(1)}, u32[]{:S(2)}, u32[]{:S(2)}) collective-permute-start(f32[512,128]{1,0:T(8,128)} %collective-permute-done.1), channel_id=1, source_target_pairs={{0,1},{1,0},{2,3},{3,2},{4,5},{5,4},{6,7},{7,6},{8,9},{9,8},{10,11... | collective-permute-start | bytes 786440 | tf_op jit(solution)/shard_map/ppermute | solution.py:37
  45.8 12.9 %collective-permute-start.4 = (f32[512,128]{1,0:T(8,128)}, f32[512,128]{1,0:T(8,128)S(1)}, u32[]{:S(2)}, u32[]{:S(2)}) collective-permute-start(f32[512,128]{1,0:T(8,128)} %collective-permute-done.3), channel_id=1, source_target_pairs={{0,1},{1,0},{2,3},{3,2},{4,5},{5,4},{6,7},{7,6},{8,9},{9,8},{10,11... | collective-permute-start | bytes 786440 | tf_op jit(solution)/shard_map/ppermute | solution.py:37
  49.6 9.5 %collective-permute-start.6 = (f32[512,128]{1,0:T(8,128)}, f32[512,128]{1,0:T(8,128)S(1)}, u32[]{:S(2)}, u32[]{:S(2)}) collective-permute-start(f32[512,128]{1,0:T(8,128)} %collective-permute-done.5), channel_id=1, source_target_pairs={{0,1},{1,0},{2,3},{3,2},{4,5},{5,4},{6,7},{7,6},{8,9},{9,8},{10,11... | collective-permute-start | bytes 786440 | tf_op jit(solution)/shard_map/ppermute | solution.py:37

commit v3 on v2

v3 whole, which is shorter than its diff:
```python
import jax
import jax.numpy as jnp
from jax import lax
from jax.experimental import pallas as pl
from jax.experimental.pallas import tpu as pltpu
from jax.sharding import PartitionSpec as P

STRIDE = 4
WINDOW_FLOPS = 10_000_000_000
PARAMS = pltpu.CompilerParams(vmem_limit_bytes=20 << 20)


def transposed_product(left, right):
    return lax.dot_general(
        left,
        right,
        (((0,), (0,)), ((), ())),
        precision=lax.Precision.HIGHEST,
        preferred_element_type=jnp.float32,
    )


def halves(array):
    high = array.astype(jnp.bfloat16)
    return high, (array - high.astype(jnp.float32)).astype(jnp.bfloat16)


def three_passes(rows, right_high, right_low):
    left_high, left_low = halves(rows.T)
    total = jnp.dot(left_high, right_high, preferred_element_type=jnp.float32)
    total += jnp.dot(left_high, right_low, preferred_element_type=jnp.float32)
    return total + jnp.dot(left_low, right_high, preferred_element_type=jnp.float32)


def first_kernel(where, rows, s_own, s_near, s_far, s_away, s_gone, out, n_high, n_low, a_high, a_low):
    columns = out.shape[1]
    part = three_passes(rows[...], *halves(s_own[...].reshape(-1, columns)))

    @pl.when(pl.program_id(0) == 0)
    def _():
        out[...] = part

    @pl.when(pl.program_id(0) > 0)
    def _():
        out[...] += part

    for index, source in enumerate((s_near, s_far)):
        n_high[index], n_low[index] = halves(source[...].reshape(-1, columns))
    for index, source in enumerate((s_away, s_gone)):
        a_high[index], a_low[index] = halves(source[...].reshape(-1, columns))


def first_product(where, rows, tiles):
    far, _, cores, panel_rows, columns = tiles.shape
    panel_columns = rows.shape[1]
    pair = cores * panel_rows

    def two(which):
        return pl.BlockSpec((None, None, cores, panel_rows, columns), lambda h, s: (h, s[which], 0, 0, 0))

    def one(which):
        return pl.BlockSpec((None, None, None, panel_rows, columns), lambda h, s: (h, s[2], s[which], 0, 0))

    def split(depth):
        shape = jax.ShapeDtypeStruct((2, far * depth, columns), jnp.bfloat16)
        return [shape] * 2, [pl.BlockSpec((2, depth, columns), lambda h, s: (0, h, 0))] * 2

    near_shapes, near_specs = split(pair)
    away_shapes, away_specs = split(panel_rows)
    return pl.pallas_call(
        first_kernel,
        out_shape=[jax.ShapeDtypeStruct((panel_columns, columns), jnp.float32)] + near_shapes + away_shapes,
        grid_spec=pltpu.PrefetchScalarGridSpec(
            num_scalar_prefetch=1,
            grid=(far,),
            in_specs=[pl.BlockSpec((pair, panel_columns), lambda h, s: (h, 0))]
            + [two(0), two(1), two(5), one(3), one(6)],
            out_specs=[pl.BlockSpec((panel_columns, columns), lambda h, s: (0, 0))] + near_specs + away_specs,
        ),
        compiler_params=PARAMS,
        cost_estimate=pl.CostEstimate(flops=WINDOW_FLOPS, bytes_accessed=8 << 20, transcendentals=0),
    )(where, rows, *[tiles] * 5)


def add_kernel(index, near, away, sofar, n_high, n_low, a_high, a_low, out):
    out[...] = (
        sofar[...]
        + three_passes(near[...], n_high[index], n_low[index])
        + three_passes(away[...], a_high[index], a_low[index])
    )


def middle_product(near, away, sofar, split):
    return pl.pallas_call(
        lambda *refs: add_kernel(0, *refs),
        out_shape=jax.ShapeDtypeStruct(sofar.shape, jnp.float32),
        compiler_params=PARAMS,
        cost_estimate=pl.CostEstimate(flops=3 << 26, bytes_accessed=3 << 20, transcendentals=0),
    )(near, away, sofar, *split)


def last_kernel(where, near, away, sofar, n_high, n_low, a_high, a_low, rhs, coupling, inverses, out, total):
    share_rows, columns = rhs.shape
    block_rows = coupling.shape[0]
    add_kernel(1, near, away, sofar, n_high, n_low, a_high, a_low, total)
    total[...] = -total[...]
    at = pl.ds(pl.multiple_of(where[4] * share_rows, share_rows), share_rows)
    total[at, :] += rhs[...]
    later = transposed_product(inverses[1], total[block_rows:, :])
    carried = total[:block_rows, :] - transposed_product(coupling[...], later)
    count = block_rows // share_rows
    out[count:] = later.reshape(count, share_rows, columns)
    out[:count] = transposed_product(inverses[0], carried).reshape(count, share_rows, columns)


def last_product(where, near, away, sofar, split, rhs, coupling, inverses):
    panel_columns, columns = sofar.shape
    share_rows = rhs.shape[0]
    out_shape = (panel_columns // share_rows, share_rows, columns)
    vmem = pl.BlockSpec(memory_space=pltpu.VMEM)
    return pl.pallas_call(
        last_kernel,
        out_shape=jax.ShapeDtypeStruct(out_shape, jnp.float32),
        in_specs=[pl.BlockSpec(memory_space=pltpu.SMEM)] + [vmem] * 10,
        scratch_shapes=[pltpu.VMEM(sofar.shape, jnp.float32)],
        compiler_params=PARAMS,
        cost_estimate=pl.CostEstimate(flops=3 << 26, bytes_accessed=3 << 20, transcendentals=0),
    )(where, near, away, sofar, *split, rhs, coupling, inverses)


def body(panel, solved, window_rhs, coupling, inverses):
    columns = window_rhs.shape[1]
    panel_rows, panel_columns = panel.shape
    grid_columns = lax.axis_size("pcol")
    chips = grid_columns // 2
    far = chips // STRIDE
    row_index = lax.axis_index("prow")
    column_index = lax.axis_index("pcol")
    core = column_index % 2
    place = (column_index // 2) % STRIDE
    tiles = solved.reshape(far, STRIDE, 2, panel_rows, columns)
    tiles = pltpu.with_memory_space_constraint(tiles, pltpu.HBM)

    def shifted(array, up, down):
        pairs = [(2 * z + c, 2 * ((z + (up, down)[c]) % chips) + c) for z in range(chips) for c in range(2)]
        return lax.ppermute(array, "pcol", pairs)

    def swapped(array):
        return lax.ppermute(array, "pcol", [(i, i ^ 1) for i in range(grid_columns)])

    groups = [[2 * (STRIDE * h + l) + c for h in range(far) for c in range(2)] for l in range(STRIDE)]
    own = lax.all_gather(panel, "pcol", axis=0, axis_index_groups=groups, tiled=True)
    near = shifted(own, 1, -1)
    by_core = own.reshape(far, 2, panel_rows, panel_columns)
    away = lax.dynamic_index_in_dim(by_core, core, 1, False).reshape(far * panel_rows, panel_columns)
    away = shifted(away, 2, -2)
    below, above = (place + STRIDE - 1) % STRIDE, (place + 1) % STRIDE
    near_place = jnp.where(core == 0, below, above)
    far_place = jnp.where(core == 0, above, below)
    where = [place, near_place, (place + 2) % STRIDE, core, row_index, far_place, 1 - core]
    where = jnp.stack(where).astype(jnp.int32)
    near, away, (sofar, *split) = lax.optimization_barrier((near, away, first_product(where, own, tiles)))
    other_near, other_away = swapped(near), swapped(away)
    sofar = middle_product(near, away, sofar, split)
    parts = last_product(where, other_near, other_away, sofar, split, window_rhs, coupling, inverses)
    return jnp.sum(lax.all_to_all(parts, "prow", 0, 0), axis=0)


def solution(mesh):
    placed = (P(("prow", "pcol"), None), P("prow", "pcol"), P("prow", "pcol"), P(), P())
    return jax.shard_map(
        body, mesh=mesh, in_specs=placed, out_specs=P("prow", "pcol"), check_vma=False
    )
```

time: 75.2 us -> 69.3 us (0.922)
  starting transfers between devices: 22.2 us -> 11.8 us
  matrix products: 7.99 us -> 0 us
  Pallas kernels: 0 us -> 6.98 us
  waiting for transfers between devices: 0.67 us -> 6.48 us
  blocking collectives: 39.3 us -> 42.8 us
  local copies, waits for them, and re-layouts: 3.54 us -> 0.13 us
    dot_general x11 -> x0, matrix products: 7.99 us -> none  [transposed_product(): lax.dot_general(left, right, (((0,), (0,)), ((), ())), precision=precisio...]
    ppermute x4 -> x2, starting transfers between devices: 13.5 us -> 5.98 us  [swapped(): lax.ppermute(array, 'pcol', [(i, i ^ 1) for i in range(grid_columns)])]
    pallas_call x0 -> x3, Pallas kernels: none -> 6.98 us  [the longest x1 4.51 us: first_product(): pl.pallas_call(first_kernel, out_shape=[jax.ShapeDtypeStruct((panel_colum...]
    ppermute x3 -> x2, waiting for transfers between devices: 0.66 us -> 5.54 us  [shifted(): return lax.ppermute(array, 'pcol', pairs)]
    all_gather x1, blocking collectives: 25.6 us -> 29.4 us  [body(): lax.all_gather(panel, 'pcol', axis=0, axis_index_groups=groups, tiled=True)]
    dynamic_slice x1, local copies, waits for them, and re-layouts: 3.51 us -> 0.02 us  [body(): lax.dynamic_index_in_dim(by_core, core, 1, False)]
    ppermute x3 -> x2, starting transfers between devices: 8.7 us -> 5.87 us  [shifted(): return lax.ppermute(array, 'pcol', pairs)]
    ppermute x4 -> x2, waiting for transfers between devices: 0.01 us -> 0.93 us  [swapped(): lax.ppermute(array, 'pcol', [(i, i ^ 1) for i in range(grid_columns)])]
  transfers between devices with their start and end apart: 7 -> 4, of which waited for: 1 -> 2; matrix products, arithmetic and copies ran while one was open for 14% -> 0% of each run, Pallas kernels for 0% -> 7%
where the time goes in v3:
time: 69.3 us; the launch traced here: 69 us
  blocking collectives  42.8 us (62%)
  starting transfers between devices  11.8 us (17%)
  Pallas kernels  6.98 us (10%)
  waiting for transfers between devices  6.48 us (9%)
    all_gather x1, blocking collectives, body(): lax.all_gather(panel, 'pcol', axis=0, axis_index_groups=groups, tiled=True)  29.4 us
    all_to_all x1, blocking collectives, body(): return jnp.sum(lax.all_to_all(parts, 'prow', 0, 0), axis=0)  13.4 us
    ppermute x2, starting transfers between devices, swapped(): lax.ppermute(array, 'pcol', [(i, i ^ 1) for i in range(grid_columns)])  5.98 us
    ppermute x2, starting transfers between devices, shifted(): return lax.ppermute(array, 'pcol', pairs)  5.87 us
    ppermute x2, waiting for transfers between devices, shifted(): return lax.ppermute(array, 'pcol', pairs)  5.54 us
    pallas_call x1, Pallas kernels, first_product(): pl.pallas_call(first_kernel, out_shape=[jax.ShapeDtypeStruct((panel_colum...  4.51 us
    pallas_call x1, Pallas kernels, last_product(): pl.pallas_call(last_kernel, out_shape=jax.ShapeDtypeStruct(out_shape, jnp...  1.91 us
  transfers between devices with their start and end apart: 4, of which 2 were waited for; matrix products, arithmetic and copies ran while one was open for 0% of the time, Pallas kernels for 7%

profile of v3, /device:TPU:1, one launch (start us, length us, event | category | flops | bytes accessed | tf_op | source)
XLA Modules:
  0.0 69.0 jit_solution(7036340643418052621)
XLA Ops:
  0.0 29.4 %all_gather.3.rows = f32[1024,128]{1,0:T(8,128)S(1)} all-gather(f32[128,128]{1,0:T(8,128)} %param.5), channel_id=1, replica_groups={{0,1,8,9,16,17,24,25},{2,3,10,11,18,19,26,27},{4,5,12,13,20,21,28,29},{..., dimensions={0}, use_global_device_ids=true | all-gather | bytes 589824 | tf_op jit(solution)/shard_map/all_gather | solution.py:152
  29.4 3.6 %collective-permute-start = (f32[1024,128]{1,0:T(8,128)S(1)}, f32[1024,128]{1,0:T(8,128)S(1)}, u32[]{:S(2)}, u32[]{:S(2)}) collective-permute-start(f32[1024,128]{1,0:T(8,128)S(1)} %all_gather.3.rows), channel_id=1, source_target_pairs={{0,2},{1,31},{2,4},{3,1},{4,6},{5,3},{6,8},{7,5},{8,10},{9,7},{10,... | collective-permute-start | bytes 1572872 | tf_op jit(solution)/shard_map/ppermute | solution.py:146
  33.1 2.2 %collective-permute-start.1 = (f32[512,128]{1,0:T(8,128)S(1)}, f32[512,128]{1,0:T(8,128)S(1)}, u32[]{:S(2)}, u32[]{:S(2)}) collective-permute-start(f32[512,128]{1,0:T(8,128)S(1)} %bitcast.13), channel_id=1, source_target_pairs={{0,4},{1,29},{2,6},{3,31},{4,8},{5,1},{6,10},{7,3},{8,12},{9,5},{1... | collective-permute-start | bytes 786440 | tf_op jit(solution)/shard_map/ppermute | solution.py:146
  35.4 0.1 stack.31.where
  35.5 4.5 %shard_map.55 = (f32[128,256]{1,0:T(8,128)S(1)}, bf16[2,1024,256]{2,1,0:T(8,128)(2,1)S(1)}, bf16[2,1024,256]{2,1,0:T(8,128)(2,1)S(1)}, bf16[2,512,256]{2,1,0:T(8,128)(2,1)S(1)}, bf16[2,512,256]{2,1,0:T(8,128)(2,1)S(1)}) custom-call(s32[7]{0:T(128)S(1)} %stack.31.where, f32[1024,128]{1,0:T(8,128)S(1)} %all_gather.3.rows, f32[4,4,2,128,256]{4,3,2,1,0:T(8,128)} %bitcast.14, ...), custom_call_target="tpu_custom_call" | custom-call | flops 10000000000 | bytes 8388608 | tf_op jit(solution)/shard_map/pallas_call | solution.py:70
  40.0 0.0 copy-start
  40.0 0.0 copy-start.1
  40.0 0.0 copy-start.2
  40.0 5.5 %collective-permute-done.1.refs_1_ = f32[512,128]{1,0:T(8,128)S(1)} collective-permute-done((f32[512,128]{1,0:T(8,128)S(1)}, f32[512,128]{1,0:T(8,128)S(1)}, u32[]{:S(2)}, u32[]{:S(2)}) %collective-permute-start.1) | collective-permute-done | bytes 262176 | tf_op jit(solution)/shard_map/ppermute | solution.py:146
  45.6 0.0 collective-permute-done.refs_0_
  45.6 4.1 %collective-permute-start.2 = (f32[1024,128]{1,0:T(8,128)S(1)}, f32[1024,128]{1,0:T(8,128)S(1)}, u32[]{:S(2)}, u32[]{:S(2)}) collective-permute-start(f32[1024,128]{1,0:T(8,128)S(1)} %collective-permute-done.refs_0_), channel_id=1, source_target_pairs={{0,1},{1,0},{2,3},{3,2},{4,5},{5,4},{6,7},{7,6},{8,9},{9,8},{10,11... | collective-permute-start | bytes 1572872 | tf_op jit(solution)/shard_map/ppermute | solution.py:149
  49.6 1.9 %collective-permute-start.3 = (f32[512,128]{1,0:T(8,128)S(1)}, f32[512,128]{1,0:T(8,128)S(1)}, u32[]{:S(2)}, u32[]{:S(2)}) collective-permute-start(f32[512,128]{1,0:T(8,128)S(1)} %collective-permute-done.1.refs_1_), channel_id=1, source_target_pairs={{0,1},{1,0},{2,3},{3,2},{4,5},{5,4},{6,7},{7,6},{8,9},{9,8},{10,11... | collective-permute-start | bytes 786440 | tf_op jit(solution)/shard_map/ppermute | solution.py:149
  51.6 0.6 shard_map.56.sofar
  52.1 0.9 %collective-permute-done.3.away = f32[512,128]{1,0:T(8,128)S(1)} collective-permute-done((f32[512,128]{1,0:T(8,128)S(1)}, f32[512,128]{1,0:T(8,128)S(1)}, u32[]{:S(2)}, u32[]{:S(2)}) %collective-permute-start.3) | collective-permute-done | bytes 262176 | tf_op jit(solution)/shard_map/ppermute | solution.py:149
  53.1 0.0 collective-permute-done.2.near
  53.1 0.0 copy-done
  53.1 0.0 copy-done.1
  53.1 0.0 copy-done.2
  53.1 1.9 %shard_map.57 = f32[16,8,256]{2,1,0:T(8,128)S(1)} custom-call(s32[7]{0:T(128)S(1)} %stack.31.where, f32[1024,128]{1,0:T(8,128)S(1)} %collective-permute-done.2.near, f32[512,128]{1,0:T(8,128)S(1)} %collective-permute-done.3.away, f32[128,256]{1,0:T(8,128)S(1)} %shard_map.56.sofar, bf16[2,1024,256]{2,1,0:T(8,128)(2,1)S(1)} %get-tuple-element.25.refs_3_.n_high, ...), custom_call_target="tpu_custom_call" | custom-call | flops 201326592 | bytes 3145728 | tf_op jit(solution)/shard_map/pallas_call | solution.py:121
  55.0 13.4 %all_to_all.5 = f32[16,8,256]{2,1,0:T(8,128)S(1)} all-to-all(f32[16,8,256]{2,1,0:T(8,128)S(1)} %shard_map.57), channel_id=1, replica_groups=mesh['prow'=16,'pcol'=32] {'prow'}, dimensions={0} | all-to-all | bytes 262144 | tf_op jit(solution)/shard_map/all_to_all | solution.py:166
  68.4 0.6 reduce_sum.9
  (1 shorter events, 0.0 us)
Async XLA Ops:
  29.4 16.2 %collective-permute-start = (f32[1024,128]{1,0:T(8,128)S(1)}, f32[1024,128]{1,0:T(8,128)S(1)}, u32[]{:S(2)}, u32[]{:S(2)}) collective-permute-start(f32[1024,128]{1,0:T(8,128)S(1)} %all_gather.3.rows), channel_id=1, source_target_pairs={{0,2},{1,31},{2,4},{3,1},{4,6},{5,3},{6,8},{7,5},{8,10},{9,7},{10,... | collective-permute-start | bytes 1572872 | tf_op jit(solution)/shard_map/ppermute | solution.py:146
  33.1 12.5 %collective-permute-start.1 = (f32[512,128]{1,0:T(8,128)S(1)}, f32[512,128]{1,0:T(8,128)S(1)}, u32[]{:S(2)}, u32[]{:S(2)}) collective-permute-start(f32[512,128]{1,0:T(8,128)S(1)} %bitcast.13), channel_id=1, source_target_pairs={{0,4},{1,29},{2,6},{3,31},{4,8},{5,1},{6,10},{7,3},{8,12},{9,5},{1... | collective-permute-start | bytes 786440 | tf_op jit(solution)/shard_map/ppermute | solution.py:146
  40.0 13.1 %copy-start = (f32[2,64,64]{2,1,0:T(8,128)S(1)}, f32[2,64,64]{2,1,0:T(8,128)}, u32[]{:S(2)}) copy-start(f32[2,64,64]{2,1,0:T(8,128)} %inverses.1) | copy-start | bytes 98308
  40.0 13.1 %copy-start.1 = (f32[64,64]{1,0:T(8,128)S(1)}, f32[64,64]{1,0:T(8,128)}, u32[]{:S(2)}) copy-start(f32[64,64]{1,0:T(8,128)} %coupling.1) | copy-start | bytes 49156
  40.0 13.1 %copy-start.2 = (f32[8,256]{1,0:T(8,128)S(1)}, f32[8,256]{1,0:T(8,128)}, u32[]{:S(2)}) copy-start(f32[8,256]{1,0:T(8,128)} %rhs.1) | copy-start | bytes 24580
  45.6 7.5 %collective-permute-start.2 = (f32[1024,128]{1,0:T(8,128)S(1)}, f32[1024,128]{1,0:T(8,128)S(1)}, u32[]{:S(2)}, u32[]{:S(2)}) collective-permute-start(f32[1024,128]{1,0:T(8,128)S(1)} %collective-permute-done.refs_0_), channel_id=1, source_target_pairs={{0,1},{1,0},{2,3},{3,2},{4,5},{5,4},{6,7},{7,6},{8,9},{9,8},{10,11... | collective-permute-start | bytes 1572872 | tf_op jit(solution)/shard_map/ppermute | solution.py:149
  49.6 3.4 %collective-permute-start.3 = (f32[512,128]{1,0:T(8,128)S(1)}, f32[512,128]{1,0:T(8,128)S(1)}, u32[]{:S(2)}, u32[]{:S(2)}) collective-permute-start(f32[512,128]{1,0:T(8,128)S(1)} %collective-permute-done.1.refs_1_), channel_id=1, source_target_pairs={{0,1},{1,0},{2,3},{3,2},{4,5},{5,4},{6,7},{7,6},{8,9},{9,8},{10,11... | collective-permute-start | bytes 786440 | tf_op jit(solution)/shard_map/ppermute | solution.py:149

commit v4 on v3

v4 whole, which is shorter than its diff:
```python
import jax
import jax.numpy as jnp
from jax import lax
from jax.experimental import pallas as pl
from jax.experimental.pallas import tpu as pltpu
from jax.sharding import PartitionSpec as P

STRIDE = 4
WINDOW_FLOPS = 10_000_000_000
PARAMS = pltpu.CompilerParams(vmem_limit_bytes=20 << 20)


def transposed_product(left, right):
    return lax.dot_general(
        left,
        right,
        (((0,), (0,)), ((), ())),
        precision=lax.Precision.HIGHEST,
        preferred_element_type=jnp.float32,
    )


def halves(array):
    high = array.astype(jnp.bfloat16)
    return high, (array - high.astype(jnp.float32)).astype(jnp.bfloat16)


def three_passes(rows, right_high, right_low):
    left_high, left_low = halves(rows.T)
    total = jnp.dot(left_high, right_high, preferred_element_type=jnp.float32)
    total += jnp.dot(left_high, right_low, preferred_element_type=jnp.float32)
    return total + jnp.dot(left_low, right_high, preferred_element_type=jnp.float32)


def plain_product(left, right):
    return jnp.dot(left, right, precision=lax.Precision.HIGHEST, preferred_element_type=jnp.float32)


def first_kernel(
    where, rows, s_own, s_near, s_far, s_away, s_gone, coupling, inverses, out, n_high, n_low, a_high, a_low, solve
):
    columns = out.shape[1]
    part = three_passes(rows[...], *halves(s_own[...].reshape(-1, columns)))

    @pl.when(pl.program_id(0) == 0)
    def _():
        out[...] = part

    @pl.when(pl.program_id(0) > 0)
    def _():
        out[...] += part

    @pl.when(pl.program_id(0) == 0)
    def _():
        upper, lower = inverses[0], inverses[1]
        carried = -plain_product(lower, plain_product(coupling[...], upper))
        top = jnp.concatenate([upper.T, carried.T], axis=1)
        bottom = jnp.concatenate([jnp.zeros_like(lower), lower.T], axis=1)
        solve[...] = jnp.concatenate([top, bottom], axis=0)

    for index, source in enumerate((s_near, s_far)):
        n_high[index], n_low[index] = halves(source[...].reshape(-1, columns))
    for index, source in enumerate((s_away, s_gone)):
        a_high[index], a_low[index] = halves(source[...].reshape(-1, columns))


def whole(array):
    return pl.BlockSpec(array.shape, lambda h, s: (0,) * array.ndim)


def first_product(where, rows, tiles, coupling, inverses):
    far, _, cores, panel_rows, columns = tiles.shape
    panel_columns = rows.shape[1]
    pair = cores * panel_rows

    def two(which):
        return pl.BlockSpec((None, None, cores, panel_rows, columns), lambda h, s: (h, s[which], 0, 0, 0))

    def one(which):
        return pl.BlockSpec((None, None, None, panel_rows, columns), lambda h, s: (h, s[2], s[which], 0, 0))

    def split(depth):
        shape = jax.ShapeDtypeStruct((2, far * depth, columns), jnp.bfloat16)
        return [shape] * 2, [pl.BlockSpec((2, depth, columns), lambda h, s: (0, h, 0))] * 2

    near_shapes, near_specs = split(pair)
    away_shapes, away_specs = split(panel_rows)
    return pl.pallas_call(
        first_kernel,
        out_shape=[jax.ShapeDtypeStruct((panel_columns, columns), jnp.float32)]
        + near_shapes
        + away_shapes
        + [jax.ShapeDtypeStruct((panel_columns, panel_columns), jnp.float32)],
        grid_spec=pltpu.PrefetchScalarGridSpec(
            num_scalar_prefetch=1,
            grid=(far,),
            in_specs=[pl.BlockSpec((pair, panel_columns), lambda h, s: (h, 0))]
            + [two(0), two(1), two(5), one(3), one(6), whole(coupling), whole(inverses)],
            out_specs=[pl.BlockSpec((panel_columns, columns), lambda h, s: (0, 0))]
            + near_specs
            + away_specs
            + [pl.BlockSpec((panel_columns, panel_columns), lambda h, s: (0, 0))],
        ),
        compiler_params=PARAMS,
        cost_estimate=pl.CostEstimate(flops=WINDOW_FLOPS, bytes_accessed=8 << 20, transcendentals=0),
    )(where, rows, *[tiles] * 5, coupling, inverses)


def call(kernel, out_shape, where, *arrays, scratch=()):
    return pl.pallas_call(
        kernel,
        out_shape=jax.ShapeDtypeStruct(out_shape, jnp.float32),
        in_specs=[pl.BlockSpec(memory_space=pltpu.SMEM)] + [pl.BlockSpec(memory_space=pltpu.VMEM)] * len(arrays),
        scratch_shapes=scratch,
        compiler_params=PARAMS,
        cost_estimate=pl.CostEstimate(flops=3 << 26, bytes_accessed=1 << 20, transcendentals=0),
    )(where, *arrays)


def middle_kernel(where, near, away, sofar, n_high, n_low, a_high, a_low, rhs, solve, out, total):
    share_rows = rhs.shape[0]
    total[...] = -sofar[...] - three_passes(near[...], n_high[0], n_low[0])
    total[...] -= three_passes(away[...], a_high[0], a_low[0])
    at = pl.ds(pl.multiple_of(where[4] * share_rows, share_rows), share_rows)
    total[at, :] += rhs[...]
    out[...] = plain_product(solve[...], total[...])


def last_kernel(where, other, sofar, n_high, n_low, a_high, a_low, solve, out):
    depth = n_high.shape[1]
    update = three_passes(other[0:depth, :], n_high[1], n_low[1])
    update += three_passes(other[depth:, :], a_high[1], a_low[1])
    out[...] = (sofar[...] - plain_product(solve[...], update)).reshape(out.shape)


def body(panel, solved, window_rhs, coupling, inverses):
    columns = window_rhs.shape[1]
    panel_rows, panel_columns = panel.shape
    grid_columns = lax.axis_size("pcol")
    chips = grid_columns // 2
    far = chips // STRIDE
    row_index = lax.axis_index("prow")
    column_index = lax.axis_index("pcol")
    core = column_index % 2
    place = (column_index // 2) % STRIDE
    tiles = solved.reshape(far, STRIDE, 2, panel_rows, columns)
    tiles = pltpu.with_memory_space_constraint(tiles, pltpu.HBM)

    def shifted(array, up, down):
        pairs = [(2 * z + c, 2 * ((z + (up, down)[c]) % chips) + c) for z in range(chips) for c in range(2)]
        return lax.ppermute(array, "pcol", pairs)

    def swapped(array):
        return lax.ppermute(array, "pcol", [(i, i ^ 1) for i in range(grid_columns)])

    groups = [[2 * (STRIDE * h + l) + c for h in range(far) for c in range(2)] for l in range(STRIDE)]
    own = lax.all_gather(panel, "pcol", axis=0, axis_index_groups=groups, tiled=True)
    near = shifted(own, 1, -1)
    by_core = own.reshape(far, 2, panel_rows, panel_columns)
    away = lax.dynamic_index_in_dim(by_core, core, 1, False).reshape(far * panel_rows, panel_columns)
    away = shifted(away, 2, -2)
    below, above = (place + STRIDE - 1) % STRIDE, (place + 1) % STRIDE
    near_place = jnp.where(core == 0, below, above)
    far_place = jnp.where(core == 0, above, below)
    where = [place, near_place, (place + 2) % STRIDE, core, row_index, far_place, 1 - core]
    where = jnp.stack(where).astype(jnp.int32)
    work = first_product(where, own, tiles, coupling, inverses)
    near, away, (sofar, *split, solve) = lax.optimization_barrier((near, away, work))
    other = swapped(jnp.concatenate([near, away]))
    shape = sofar.shape
    sofar = call(
        middle_kernel, shape, where, near, away, sofar, *split, window_rhs, solve,
        scratch=[pltpu.VMEM(shape, jnp.float32)],
    )
    parts_shape = (shape[0] // window_rhs.shape[0],) + window_rhs.shape
    parts = call(last_kernel, parts_shape, where, other, sofar, *split, solve)
    return jnp.sum(lax.all_to_all(parts, "prow", 0, 0), axis=0)


def solution(mesh):
    placed = (P(("prow", "pcol"), None), P("prow", "pcol"), P("prow", "pcol"), P(), P())
    return jax.shard_map(
        body, mesh=mesh, in_specs=placed, out_specs=P("prow", "pcol"), check_vma=False
    )
```

time: 69.3 us -> 67.5 us (0.974)
  waiting for transfers between devices: 6.48 us -> 3.85 us
  starting transfers between devices: 11.8 us -> 9.94 us
  local copies, waits for them, and re-layouts: 0.13 us -> 1.71 us
  Pallas kernels: 6.98 us -> 8.02 us
    ppermute x2, waiting for transfers between devices: 5.54 us -> 3.48 us  [shifted(): return lax.ppermute(array, 'pcol', pairs)]
    ppermute x2 -> x1, starting transfers between devices: 5.98 us -> 4.07 us  [swapped(): lax.ppermute(array, 'pcol', [(i, i ^ 1) for i in range(grid_columns)])]
    unnamed x6, local copies, waits for them, and re-layouts: 0.02 us -> 1.6 us
  transfers between devices with their start and end apart: 4 -> 3, of which waited for: 2 -> 2; matrix products, arithmetic and copies ran while one was open for 0% -> 0% of each run, Pallas kernels for 7% -> 10%
where the time goes in v4:
time: 67.5 us; the launch traced here: 67.1 us
  blocking collectives  42.8 us (63%)
  starting transfers between devices  9.94 us (15%)
  Pallas kernels  8.02 us (12%)
  waiting for transfers between devices  3.85 us (6%)
  local copies, waits for them, and re-layouts  1.71 us (3%)
    all_gather x1, blocking collectives, body(): lax.all_gather(panel, 'pcol', axis=0, axis_index_groups=groups, tiled=True)  29.4 us
    all_to_all x1, blocking collectives, body(): return jnp.sum(lax.all_to_all(parts, 'prow', 0, 0), axis=0)  13.4 us
    ppermute x2, starting transfers between devices, shifted(): return lax.ppermute(array, 'pcol', pairs)  5.87 us
    pallas_call x1, Pallas kernels, first_product(): pl.pallas_call(first_kernel, out_shape=[jax.ShapeDtypeStruct((panel_colum...  5 us
    ppermute x1, starting transfers between devices, swapped(): lax.ppermute(array, 'pcol', [(i, i ^ 1) for i in range(grid_columns)])  4.07 us
    ppermute x2, waiting for transfers between devices, shifted(): return lax.ppermute(array, 'pcol', pairs)  3.48 us
    pallas_call x2, Pallas kernels, call(): pl.pallas_call(kernel, out_shape=jax.ShapeDtypeStruct(out_shape, jnp.floa...  3.01 us
    unnamed x6, local copies, waits for them, and re-layouts  1.6 us
  transfers between devices with their start and end apart: 3, of which 2 were waited for; matrix products, arithmetic and copies ran while one was open for 0% of the time, Pallas kernels for 10%

profile of v4, /device:TPU:1, one launch (start us, length us, event | category | flops | bytes accessed | tf_op | source)
XLA Modules:
  0.0 67.1 jit_solution(18001883040921996832)
XLA Ops:
  0.0 29.4 %all_gather.3.rows = f32[1024,128]{1,0:T(8,128)S(1)} all-gather(f32[128,128]{1,0:T(8,128)} %param.5), channel_id=1, replica_groups={{0,1,8,9,16,17,24,25},{2,3,10,11,18,19,26,27},{4,5,12,13,20,21,28,29},{..., dimensions={0}, use_global_device_ids=true | all-gather | bytes 589824 | tf_op jit(solution)/shard_map/all_gather | solution.py:157
  29.4 3.6 %collective-permute-start = (f32[1024,128]{1,0:T(8,128)S(1)}, f32[1024,128]{1,0:T(8,128)S(1)}, u32[]{:S(2)}, u32[]{:S(2)}) collective-permute-start(f32[1024,128]{1,0:T(8,128)S(1)} %all_gather.3.rows), channel_id=1, source_target_pairs={{0,2},{1,31},{2,4},{3,1},{4,6},{5,3},{6,8},{7,5},{8,10},{9,7},{10,... | collective-permute-start | bytes 1572872 | tf_op jit(solution)/shard_map/ppermute | solution.py:151
  33.1 2.2 %collective-permute-start.1 = (f32[512,128]{1,0:T(8,128)S(1)}, f32[512,128]{1,0:T(8,128)S(1)}, u32[]{:S(2)}, u32[]{:S(2)}) collective-permute-start(f32[512,128]{1,0:T(8,128)S(1)} %bitcast.13), channel_id=1, source_target_pairs={{0,4},{1,29},{2,6},{3,31},{4,8},{5,1},{6,10},{7,3},{8,12},{9,5},{1... | collective-permute-start | bytes 786440 | tf_op jit(solution)/shard_map/ppermute | solution.py:151
  35.4 0.1 stack.31.where
  35.5 0.0 copy-start.1
  35.5 0.8 %copy-done.1 = f32[2,64,64]{2,1,0:T(8,128)S(1)} copy-done((f32[2,64,64]{2,1,0:T(8,128)S(1)}, f32[2,64,64]{2,1,0:T(8,128)}, u32[]{:S(2)}) %copy-start.1) | copy-done | bytes 32792
  36.3 0.0 copy-start.2
  36.3 0.8 %copy-done.2 = f32[64,64]{1,0:T(8,128)S(1)} copy-done((f32[64,64]{1,0:T(8,128)S(1)}, f32[64,64]{1,0:T(8,128)}, u32[]{:S(2)}) %copy-start.2) | copy-done | bytes 16408
  37.1 0.0 copy-start
  37.1 5.0 %shard_map.55 = (f32[128,256]{1,0:T(8,128)S(1)}, bf16[2,1024,256]{2,1,0:T(8,128)(2,1)S(1)}, bf16[2,1024,256]{2,1,0:T(8,128)(2,1)S(1)}, bf16[2,512,256]{2,1,0:T(8...) custom-call(s32[7]{0:T(128)S(1)} %stack.31.where, f32[1024,128]{1,0:T(8,128)S(1)} %all_gather.3.rows, ...), custom_call_target="tpu_custom_call" | custom-call | flops 10000000000 | bytes 8388608 | tf_op jit(solution)/shard_map/pallas_call | solution.py:88
  42.1 3.5 %collective-permute-done.1.away = f32[512,128]{1,0:T(8,128)S(1)} collective-permute-done((f32[512,128]{1,0:T(8,128)S(1)}, f32[512,128]{1,0:T(8,128)S(1)}, u32[]{:S(2)}, u32[]{:S(2)}) %collective-permute-start.1) | collective-permute-done | bytes 262176 | tf_op jit(solution)/shard_map/ppermute | solution.py:151
  45.6 0.0 collective-permute-done.near
  45.6 0.1 pad_maximum_fusion
  45.6 4.1 %collective-permute-start.2 = (f32[1536,128]{1,0:T(8,128)S(1)}, f32[1536,128]{1,0:T(8,128)S(1)}, u32[]{:S(2)}, u32[]{:S(2)}) collective-permute-start(f32[1536,128]{1,0:T(8,128)S(1)} %pad_maximum_fusion), channel_id=1, source_target_pairs={{0,1},{1,0},{2,3},{3,2},{4,5},{5,4},{6,7},{7,6},{8,9},{9,8},{10,11... | collective-permute-start | bytes 2359304 | tf_op jit(solution)/shard_map/ppermute | solution.py:154
  49.7 0.0 copy-done
  49.7 1.5 %shard_map.56.sofar = f32[128,256]{1,0:T(8,128)S(1)} custom-call(s32[7]{0:T(128)S(1)} %stack.31.where, f32[1024,128]{1,0:T(8,128)S(1)} %collective-permute-done.near, f32[512,128]{1,0:T(8,128)S(1)} %collective-permute-done.1.away, f32[128,256]{1,0:T(8,128)S(1)} %get-tuple-element.27.sofar, bf16[2,1024,256]{2,1,0:T(8,128)(2,1)S(1)} %get-tuple-element.28.n_high, ...), custom_call_target="tpu_custom_call" | custom-call | flops 201326592 | bytes 1048576 | tf_op jit(solution)/shard_map/pallas_call | solution.py:110
  51.2 0.4 collective-permute-done.2.other
  51.6 1.5 %shard_map.57 = f32[16,8,256]{2,1,0:T(8,128)S(1)} custom-call(s32[7]{0:T(128)S(1)} %stack.31.where, f32[1536,128]{1,0:T(8,128)S(1)} %collective-permute-done.2.other, f32[128,256]{1,0:T(8,128)S(1)} %shard_map.56.sofar, bf16[2,1024,256]{2,1,0:T(8,128)(2,1)S(1)} %get-tuple-element.28.n_high, bf16[2,1024,256]{2,1,0:T(8,128)(2,1)S(1)} %get-tuple-element.29.n_low, ...), custom_call_target="tpu_custom_call" | custom-call | flops 201326592 | bytes 1048576 | tf_op jit(solution)/shard_map/pallas_call | solution.py:110
  53.1 13.4 %all_to_all.5 = f32[16,8,256]{2,1,0:T(8,128)S(1)} all-to-all(f32[16,8,256]{2,1,0:T(8,128)S(1)} %shard_map.57), channel_id=1, replica_groups=mesh['prow'=16,'pcol'=32] {'prow'}, dimensions={0} | all-to-all | bytes 262144 | tf_op jit(solution)/shard_map/all_to_all | solution.py:177
  66.5 0.6 reduce_sum.9
  (1 shorter events, 0.0 us)
Async XLA Ops:
  29.4 16.2 %collective-permute-start = (f32[1024,128]{1,0:T(8,128)S(1)}, f32[1024,128]{1,0:T(8,128)S(1)}, u32[]{:S(2)}, u32[]{:S(2)}) collective-permute-start(f32[1024,128]{1,0:T(8,128)S(1)} %all_gather.3.rows), channel_id=1, source_target_pairs={{0,2},{1,31},{2,4},{3,1},{4,6},{5,3},{6,8},{7,5},{8,10},{9,7},{10,... | collective-permute-start | bytes 1572872 | tf_op jit(solution)/shard_map/ppermute | solution.py:151
  33.1 12.5 %collective-permute-start.1 = (f32[512,128]{1,0:T(8,128)S(1)}, f32[512,128]{1,0:T(8,128)S(1)}, u32[]{:S(2)}, u32[]{:S(2)}) collective-permute-start(f32[512,128]{1,0:T(8,128)S(1)} %bitcast.13), channel_id=1, source_target_pairs={{0,4},{1,29},{2,6},{3,31},{4,8},{5,1},{6,10},{7,3},{8,12},{9,5},{1... | collective-permute-start | bytes 786440 | tf_op jit(solution)/shard_map/ppermute | solution.py:151
  35.5 0.8 %copy-start.1 = (f32[2,64,64]{2,1,0:T(8,128)S(1)}, f32[2,64,64]{2,1,0:T(8,128)}, u32[]{:S(2)}) copy-start(f32[2,64,64]{2,1,0:T(8,128)} %inverses.1) | copy-start | bytes 98308
  36.3 0.8 %copy-start.2 = (f32[64,64]{1,0:T(8,128)S(1)}, f32[64,64]{1,0:T(8,128)}, u32[]{:S(2)}) copy-start(f32[64,64]{1,0:T(8,128)} %coupling.1) | copy-start | bytes 49156
  37.1 12.6 %copy-start = (f32[8,256]{1,0:T(8,128)S(1)}, f32[8,256]{1,0:T(8,128)}, u32[]{:S(2)}) copy-start(f32[8,256]{1,0:T(8,128)} %rhs.1) | copy-start | bytes 24580
  45.6 6.0 %collective-permute-start.2 = (f32[1536,128]{1,0:T(8,128)S(1)}, f32[1536,128]{1,0:T(8,128)S(1)}, u32[]{:S(2)}, u32[]{:S(2)}) collective-permute-start(f32[1536,128]{1,0:T(8,128)S(1)} %pad_maximum_fusion), channel_id=1, source_target_pairs={{0,1},{1,0},{2,3},{3,2},{4,5},{5,4},{6,7},{7,6},{8,9},{9,8},{10,11... | collective-permute-start | bytes 2359304 | tf_op jit(solution)/shard_map/ppermute | solution.py:154

commit v5 on v4

v5 whole, which is shorter than its diff:
```python
import jax
import jax.numpy as jnp
from jax import lax
from jax.experimental import pallas as pl
from jax.experimental.pallas import tpu as pltpu
from jax.sharding import PartitionSpec as P

STRIDE = 4
WINDOW_FLOPS = 10_000_000_000
PARAMS = pltpu.CompilerParams(vmem_limit_bytes=20 << 20)


def plain_product(left, right):
    return jnp.dot(left, right, precision=lax.Precision.HIGHEST, preferred_element_type=jnp.float32)


def halves(array):
    high = array.astype(jnp.bfloat16)
    return high, (array - high.astype(jnp.float32)).astype(jnp.bfloat16)


def three_passes(rows, right_high, right_low):
    left_high, left_low = halves(rows.T)
    total = jnp.dot(left_high, right_high, preferred_element_type=jnp.float32)
    total += jnp.dot(left_high, right_low, preferred_element_type=jnp.float32)
    return total + jnp.dot(left_low, right_high, preferred_element_type=jnp.float32)


def first_kernel(where, rows, tiles, coupling, inverses, out, own_high, own_low, other_high, other_low, solve):
    core = where[4]
    part = three_passes(rows[...], *halves(tiles[where[0], core]))

    @pl.when(pl.program_id(0) == 0)
    def _():
        out[...] = part
        upper, lower = inverses[0], inverses[1]
        carried = -plain_product(lower, plain_product(coupling[...], upper))
        top = jnp.concatenate([upper.T, carried.T], axis=1)
        bottom = jnp.concatenate([jnp.zeros_like(lower), lower.T], axis=1)
        solve[...] = jnp.concatenate([top, bottom], axis=0)

    @pl.when(pl.program_id(0) > 0)
    def _():
        out[...] += part

    for index in range(STRIDE):
        if index:
            own_high[index - 1], own_low[index - 1] = halves(tiles[where[index], core])
        other_high[index], other_low[index] = halves(tiles[where[index], 1 - core])


def first_product(where, rows, tiles, coupling, inverses):
    far, _, cores, panel_rows, columns = tiles.shape
    panel_columns = rows.shape[1]

    def whole(shape):
        return pl.BlockSpec(shape, lambda h, s: (0,) * len(shape))

    def split(count):
        shape = jax.ShapeDtypeStruct((count, far * panel_rows, columns), jnp.bfloat16)
        return [shape] * 2, [pl.BlockSpec((count, panel_rows, columns), lambda h, s: (0, h, 0))] * 2

    own_shapes, own_specs = split(STRIDE - 1)
    other_shapes, other_specs = split(STRIDE)
    product, square = (panel_columns, columns), (panel_columns, panel_columns)
    return pl.pallas_call(
        first_kernel,
        out_shape=[jax.ShapeDtypeStruct(product, jnp.float32)]
        + own_shapes
        + other_shapes
        + [jax.ShapeDtypeStruct(square, jnp.float32)],
        grid_spec=pltpu.PrefetchScalarGridSpec(
            num_scalar_prefetch=1,
            grid=(far,),
            in_specs=[
                pl.BlockSpec((panel_rows, panel_columns), lambda h, s: (h, 0)),
                pl.BlockSpec((None, STRIDE, cores, panel_rows, columns), lambda h, s: (h, 0, 0, 0, 0)),
                whole(coupling.shape),
                whole(inverses.shape),
            ],
            out_specs=[whole(product)] + own_specs + other_specs + [whole(square)],
        ),
        compiler_params=PARAMS,
        cost_estimate=pl.CostEstimate(flops=WINDOW_FLOPS, bytes_accessed=8 << 20, transcendentals=0),
    )(where, rows, tiles, coupling, inverses)


def call(kernel, out_shape, where, *arrays, scratch=()):
    return pl.pallas_call(
        kernel,
        out_shape=jax.ShapeDtypeStruct(out_shape, jnp.float32),
        in_specs=[pl.BlockSpec(memory_space=pltpu.SMEM)] + [pl.BlockSpec(memory_space=pltpu.VMEM)] * len(arrays),
        scratch_shapes=scratch,
        compiler_params=PARAMS,
        cost_estimate=pl.CostEstimate(flops=3 << 26, bytes_accessed=1 << 20, transcendentals=0),
    )(where, *arrays)


def middle_kernel(where, up, down, away, sofar, own_high, own_low, rhs, solve, out, total):
    share_rows = rhs.shape[0]
    total[...] = -sofar[...]
    for index, rows in enumerate((up, down, away)):
        total[...] -= three_passes(rows[...], own_high[index], own_low[index])
    at = pl.ds(pl.multiple_of(where[5] * share_rows, share_rows), share_rows)
    total[at, :] += rhs[...]
    out[...] = plain_product(solve[...], total[...])


def last_kernel(where, rows, sofar, other_high, other_low, solve, out):
    columns = sofar.shape[1]
    right = [half[...].reshape(-1, columns) for half in (other_high, other_low)]
    update = three_passes(rows[...], *right)
    out[...] = (sofar[...] - plain_product(solve[...], update)).reshape(out.shape)


def body(panel, solved, window_rhs, coupling, inverses):
    share_rows, columns = window_rhs.shape
    panel_rows, panel_columns = panel.shape
    grid_columns = lax.axis_size("pcol")
    chips = grid_columns // 2
    far = chips // STRIDE
    row_index = lax.axis_index("prow")
    column_index = lax.axis_index("pcol")
    place = (column_index // 2) % STRIDE
    tiles = solved.reshape(far, STRIDE, 2, panel_rows, columns)
    tiles, coupling, inverses = (
        pltpu.with_memory_space_constraint(array, pltpu.HBM) for array in (tiles, coupling, inverses)
    )

    def shifted(array, up, down):
        pairs = [(2 * z + c, 2 * ((z + (up, down)[c]) % chips) + c) for z in range(chips) for c in range(2)]
        return lax.ppermute(array, "pcol", pairs)

    def swapped(array):
        return lax.ppermute(array, "pcol", [(i, i ^ 1) for i in range(grid_columns)])

    groups = [[2 * (STRIDE * h + l) + c for h in range(far)] for l in range(STRIDE) for c in range(2)]
    own = lax.all_gather(panel, "pcol", axis=0, axis_index_groups=groups, tiled=True)
    first = shifted(own, 1, -1)
    second = shifted(own, -1, 1)
    away = shifted(own, 2, -2)
    core = column_index % 2
    below, above = (place + STRIDE - 1) % STRIDE, (place + 1) % STRIDE
    firsts = [jnp.where(core == 0, below, above), jnp.where(core == 0, above, below)]
    where = jnp.stack([place, *firsts, (place + 2) % STRIDE, core, row_index]).astype(jnp.int32)
    work = first_product(where, own, tiles, coupling, inverses)
    first, second, away, work = lax.optimization_barrier((first, second, away, work))
    sofar, own_high, own_low, other_high, other_low, solve = work
    other = swapped(jnp.concatenate([own, second, first, away]))
    shape = sofar.shape
    sofar = call(
        middle_kernel, shape, where, first, second, away, sofar, own_high, own_low, window_rhs, solve,
        scratch=[pltpu.VMEM(shape, jnp.float32)],
    )
    parts_shape = (shape[0] // share_rows, share_rows, columns)
    parts = call(last_kernel, parts_shape, where, other, sofar, other_high, other_low, solve)
    return jnp.sum(lax.all_to_all(parts, "prow", 0, 0), axis=0)


def solution(mesh):
    placed = (P(("prow", "pcol"), None), P("prow", "pcol"), P("prow", "pcol"), P(), P())
    return jax.shard_map(
        body, mesh=mesh, in_specs=placed, out_specs=P("prow", "pcol"), check_vma=False
    )
```

time: 67.5 us -> 65.9 us (0.976)
  starting transfers between devices: 9.94 us -> 14.8 us
  blocking collectives: 42.8 us -> 38.9 us
  local copies, waits for them, and re-layouts: 1.71 us -> 0.09 us
  waiting for transfers between devices: 3.85 us -> 2.84 us
    all_gather x1, blocking collectives: 29.4 us -> 25.5 us  [body(): lax.all_gather(panel, 'pcol', axis=0, axis_index_groups=groups, tiled=True)]
    ppermute x2 -> x3, starting transfers between devices: 5.87 us -> 9.21 us  [shifted(): return lax.ppermute(array, 'pcol', pairs)]
    unnamed x6 -> x2, local copies, waits for them, and re-layouts: 1.6 us -> 0.01 us
    ppermute x1, starting transfers between devices: 4.07 us -> 5.63 us  [swapped(): lax.ppermute(array, 'pcol', [(i, i ^ 1) for i in range(grid_columns)])]
    ppermute x2 -> x3, waiting for transfers between devices: 3.48 us -> 2.11 us  [shifted(): return lax.ppermute(array, 'pcol', pairs)]
  transfers between devices with their start and end apart: 3 -> 4, of which waited for: 2 -> 3; matrix products, arithmetic and copies ran while one was open for 0% -> 0% of each run, Pallas kernels for 10% -> 10%
where the time goes in v5:
time: 65.9 us; the launch traced here: 65.6 us
  blocking collectives  38.9 us (59%)
  starting transfers between devices  14.8 us (22%)
  Pallas kernels  8.09 us (12%)
  waiting for transfers between devices  2.84 us (4%)
  other arithmetic  0.68 us (1%)
    all_gather x1, blocking collectives, body(): lax.all_gather(panel, 'pcol', axis=0, axis_index_groups=groups, tiled=True)  25.5 us
    all_to_all x1, blocking collectives, body(): return jnp.sum(lax.all_to_all(parts, 'prow', 0, 0), axis=0)  13.4 us
    ppermute x3, starting transfers between devices, shifted(): return lax.ppermute(array, 'pcol', pairs)  9.21 us
    ppermute x1, starting transfers between devices, swapped(): lax.ppermute(array, 'pcol', [(i, i ^ 1) for i in range(grid_columns)])  5.63 us
    pallas_call x1, Pallas kernels, first_product(): pl.pallas_call(first_kernel, out_shape=[jax.ShapeDtypeStruct(product, jnp...  4.92 us
    pallas_call x2, Pallas kernels, call(): pl.pallas_call(kernel, out_shape=jax.ShapeDtypeStruct(out_shape, jnp.floa...  3.17 us
    ppermute x3, waiting for transfers between devices, shifted(): return lax.ppermute(array, 'pcol', pairs)  2.11 us
  transfers between devices with their start and end apart: 4, of which 3 were waited for; matrix products, arithmetic and copies ran while one was open for 0% of the time, Pallas kernels for 10%

profile of v5, /device:TPU:1, one launch (start us, length us, event | category | flops | bytes accessed | tf_op | source)
XLA Modules:
  0.0 65.6 jit_solution(10111531804855016581)
XLA Ops:
  0.0 25.5 %all_gather.3.rows = f32[512,128]{1,0:T(8,128)S(1)} all-gather(f32[128,128]{1,0:T(8,128)} %param.5), channel_id=1, replica_groups={{0,8,16,24},{1,9,17,25},{2,10,18,26},{3,11,19,27},{4,12,20,28},{5,13,21..., dimensions={0}, use_global_device_ids=true | all-gather | bytes 327680 | tf_op jit(solution)/shard_map/all_gather | solution.py:138
  25.5 2.7 %collective-permute-start.2 = (f32[512,128]{1,0:T(8,128)S(1)}, f32[512,128]{1,0:T(8,128)S(1)}, u32[]{:S(2)}, u32[]{:S(2)}) collective-permute-start(f32[512,128]{1,0:T(8,128)S(1)} %all_gather.3.rows), channel_id=1, source_target_pairs={{0,4},{1,29},{2,6},{3,31},{4,8},{5,1},{6,10},{7,3},{8,12},{9,5},{1... | collective-permute-start | bytes 786440 | tf_op jit(solution)/shard_map/ppermute | solution.py:132
  28.2 3.7 %collective-permute-start.1 = (f32[512,128]{1,0:T(8,128)S(1)}, f32[512,128]{1,0:T(8,128)S(1)}, u32[]{:S(2)}, u32[]{:S(2)}) collective-permute-start(f32[512,128]{1,0:T(8,128)S(1)} %all_gather.3.rows), channel_id=1, source_target_pairs={{0,30},{1,3},{2,0},{3,5},{4,2},{5,7},{6,4},{7,9},{8,6},{9,11},{10,... | collective-permute-start | bytes 786440 | tf_op jit(solution)/shard_map/ppermute | solution.py:132
  31.8 2.8 %collective-permute-start = (f32[512,128]{1,0:T(8,128)S(1)}, f32[512,128]{1,0:T(8,128)S(1)}, u32[]{:S(2)}, u32[]{:S(2)}) collective-permute-start(f32[512,128]{1,0:T(8,128)S(1)} %all_gather.3.rows), channel_id=1, source_target_pairs={{0,2},{1,31},{2,4},{3,1},{4,6},{5,3},{6,8},{7,5},{8,10},{9,7},{10,... | collective-permute-start | bytes 786440 | tf_op jit(solution)/shard_map/ppermute | solution.py:132
  34.8 0.1 stack.27.where
  34.9 0.0 copy-start
  34.9 4.9 %shard_map.55 = (f32[128,256]{1,0:T(8,128)S(1)}, bf16[3,512,256]{2,1,0:T(8,128)(2,1)S(1)}, bf16[3,512,256]{2,1,0:T(8,128)(2,1)S(1)}, bf16[4,512,256]{2,1,0:T(8,1...) custom-call(s32[6]{0:T(128)S(1)} %stack.27.where, f32[512,128]{1,0:T(8,128)S(1)} %all_gather.3.rows, ...), custom_call_target="tpu_custom_call" | custom-call | flops 10000000000 | bytes 8388608 | tf_op jit(solution)/shard_map/pallas_call | solution.py:66
  39.8 0.0 collective-permute-done.2.away
  39.8 1.0 %collective-permute-done.1.down = f32[512,128]{1,0:T(8,128)S(1)} collective-permute-done((f32[512,128]{1,0:T(8,128)S(1)}, f32[512,128]{1,0:T(8,128)S(1)}, u32[]{:S(2)}, u32[]{:S(2)}) %collective-permute-start.1) | collective-permute-done | bytes 262176 | tf_op jit(solution)/shard_map/ppermute | solution.py:132
  40.8 1.1 %collective-permute-done.up = f32[512,128]{1,0:T(8,128)S(1)} collective-permute-done((f32[512,128]{1,0:T(8,128)S(1)}, f32[512,128]{1,0:T(8,128)S(1)}, u32[]{:S(2)}, u32[]{:S(2)}) %collective-permute-start) | collective-permute-done | bytes 262176 | tf_op jit(solution)/shard_map/ppermute | solution.py:132
  41.9 0.1 pad_maximum_fusion
  42.0 5.6 %collective-permute-start.3 = (f32[2048,128]{1,0:T(8,128)S(1)}, f32[2048,128]{1,0:T(8,128)S(1)}, u32[]{:S(2)}, u32[]{:S(2)}) collective-permute-start(f32[2048,128]{1,0:T(8,128)S(1)} %pad_maximum_fusion), channel_id=1, source_target_pairs={{0,1},{1,0},{2,3},{3,2},{4,5},{5,4},{6,7},{7,6},{8,9},{9,8},{10,11... | collective-permute-start | bytes 3145736 | tf_op jit(solution)/shard_map/ppermute | solution.py:135
  47.6 0.0 copy-done
  47.6 1.5 %shard_map.56.sofar = f32[128,256]{1,0:T(8,128)S(1)} custom-call(s32[6]{0:T(128)S(1)} %stack.27.where, f32[512,128]{1,0:T(8,128)S(1)} %collective-permute-done.up, f32[512,128]{1,0:T(8,128)S(1)} %collective-permute-done.1.down, f32[512,128]{1,0:T(8,128)S(1)} %collective-permute-done.2.away, f32[128,256]{1,0:T(8,128)S(1)} %get-tuple-element.29.sofar, ...), custom_call_target="tpu_custom_call" | custom-call | flops 201326592 | bytes 1048576 | tf_op jit(solution)/shard_map/pallas_call | solution.py:89
  49.1 0.7 %collective-permute-done.3.rows = f32[2048,128]{1,0:T(8,128)S(1)} collective-permute-done((f32[2048,128]{1,0:T(8,128)S(1)}, f32[2048,128]{1,0:T(8,128)S(1)}, u32[]{:S(2)}, u32[]{:S(2)}) %collective-permute-start.3) | collective-permute-done | bytes 1048608 | tf_op jit(solution)/shard_map/ppermute | solution.py:135
  49.9 1.7 %shard_map.57 = f32[16,8,256]{2,1,0:T(8,128)S(1)} custom-call(s32[6]{0:T(128)S(1)} %stack.27.where, f32[2048,128]{1,0:T(8,128)S(1)} %collective-permute-done.3.rows, f32[128,256]{1,0:T(8,128)S(1)} %shard_map.56.sofar, bf16[4,512,256]{2,1,0:T(8,128)(2,1)S(1)} %get-tuple-element.33.other_high, bf16[4,512,256]{2,1,0:T(8,128)(2,1)S(1)} %get-tuple-element.34.other_low, ...), custom_call_target="tpu_custom_call" | custom-call | flops 201326592 | bytes 1048576 | tf_op jit(solution)/shard_map/pallas_call | solution.py:89
  51.5 13.4 %all_to_all.5 = f32[16,8,256]{2,1,0:T(8,128)S(1)} all-to-all(f32[16,8,256]{2,1,0:T(8,128)S(1)} %shard_map.57), channel_id=1, replica_groups=mesh['prow'=16,'pcol'=32] {'prow'}, dimensions={0} | all-to-all | bytes 262144 | tf_op jit(solution)/shard_map/all_to_all | solution.py:157
  64.9 0.6 reduce_sum.9
Async XLA Ops:
  25.5 14.3 %collective-permute-start.2 = (f32[512,128]{1,0:T(8,128)S(1)}, f32[512,128]{1,0:T(8,128)S(1)}, u32[]{:S(2)}, u32[]{:S(2)}) collective-permute-start(f32[512,128]{1,0:T(8,128)S(1)} %all_gather.3.rows), channel_id=1, source_target_pairs={{0,4},{1,29},{2,6},{3,31},{4,8},{5,1},{6,10},{7,3},{8,12},{9,5},{1... | collective-permute-start | bytes 786440 | tf_op jit(solution)/shard_map/ppermute | solution.py:132
  28.2 12.6 %collective-permute-start.1 = (f32[512,128]{1,0:T(8,128)S(1)}, f32[512,128]{1,0:T(8,128)S(1)}, u32[]{:S(2)}, u32[]{:S(2)}) collective-permute-start(f32[512,128]{1,0:T(8,128)S(1)} %all_gather.3.rows), channel_id=1, source_target_pairs={{0,30},{1,3},{2,0},{3,5},{4,2},{5,7},{6,4},{7,9},{8,6},{9,11},{10,... | collective-permute-start | bytes 786440 | tf_op jit(solution)/shard_map/ppermute | solution.py:132
  31.8 10.1 %collective-permute-start = (f32[512,128]{1,0:T(8,128)S(1)}, f32[512,128]{1,0:T(8,128)S(1)}, u32[]{:S(2)}, u32[]{:S(2)}) collective-permute-start(f32[512,128]{1,0:T(8,128)S(1)} %all_gather.3.rows), channel_id=1, source_target_pairs={{0,2},{1,31},{2,4},{3,1},{4,6},{5,3},{6,8},{7,5},{8,10},{9,7},{10,... | collective-permute-start | bytes 786440 | tf_op jit(solution)/shard_map/ppermute | solution.py:132
  34.9 12.8 %copy-start = (f32[8,256]{1,0:T(8,128)S(1)}, f32[8,256]{1,0:T(8,128)}, u32[]{:S(2)}) copy-start(f32[8,256]{1,0:T(8,128)} %rhs.1) | copy-start | bytes 24580
  42.0 7.9 %collective-permute-start.3 = (f32[2048,128]{1,0:T(8,128)S(1)}, f32[2048,128]{1,0:T(8,128)S(1)}, u32[]{:S(2)}, u32[]{:S(2)}) collective-permute-start(f32[2048,128]{1,0:T(8,128)S(1)} %pad_maximum_fusion), channel_id=1, source_target_pairs={{0,1},{1,0},{2,3},{3,2},{4,5},{5,4},{6,7},{7,6},{8,9},{9,8},{10,11... | collective-permute-start | bytes 3145736 | tf_op jit(solution)/shard_map/ppermute | solution.py:135

commit v6 on v5

v6 whole, which is shorter than its diff:
```python
import jax
import jax.numpy as jnp
from jax import lax
from jax.experimental import pallas as pl
from jax.experimental.pallas import tpu as pltpu
from jax.sharding import PartitionSpec as P

STRIDE = 4
WINDOW_FLOPS = 10_000_000_000
PARAMS = pltpu.CompilerParams(vmem_limit_bytes=20 << 20)


def plain_product(left, right):
    return jnp.dot(left, right, precision=lax.Precision.HIGHEST, preferred_element_type=jnp.float32)


def halves(array):
    high = array.astype(jnp.bfloat16)
    return high, (array - high.astype(jnp.float32)).astype(jnp.bfloat16)


def three_passes(rows, right_high, right_low):
    left_high, left_low = halves(rows.T)
    total = jnp.dot(left_high, right_high, preferred_element_type=jnp.float32)
    total += jnp.dot(left_high, right_low, preferred_element_type=jnp.float32)
    return total + jnp.dot(left_low, right_high, preferred_element_type=jnp.float32)


def split_kernel(where, tiles, coupling, inverses, high, low, solve, held, sems):
    far, stride, cores = tiles.shape[:3]
    copies = [pltpu.make_async_copy(tiles.at[h], held.at[h], sems.at[h]) for h in range(far)]
    for copy in copies:
        copy.start()
    upper, lower = inverses[0], inverses[1]
    carried = -plain_product(lower, plain_product(coupling[...], upper))
    top = jnp.concatenate([upper.T, carried.T], axis=1)
    bottom = jnp.concatenate([jnp.zeros_like(lower), lower.T], axis=1)
    solve[...] = jnp.concatenate([top, bottom], axis=0)
    for h in range(far):
        copies[h].wait()

        def one(index, _, h=h):
            at = (h, index // cores, index % cores)
            high[at], low[at] = halves(held[at])
            return 0

        lax.fori_loop(0, stride * cores, one, 0)


def split(where, tiles, coupling, inverses):
    block_rows = coupling.shape[0]
    half = jax.ShapeDtypeStruct(tiles.shape, jnp.bfloat16)
    vmem = pl.BlockSpec(memory_space=pltpu.VMEM)
    return pl.pallas_call(
        split_kernel,
        out_shape=[half, half, jax.ShapeDtypeStruct((2 * block_rows, 2 * block_rows), jnp.float32)],
        in_specs=[pl.BlockSpec(memory_space=pltpu.SMEM), pl.BlockSpec(memory_space=pltpu.HBM), vmem, vmem],
        out_specs=[vmem] * 3,
        scratch_shapes=[pltpu.VMEM(tiles.shape, jnp.float32), pltpu.SemaphoreType.DMA(tiles.shape[:1])],
        compiler_params=PARAMS,
        cost_estimate=pl.CostEstimate(flops=WINDOW_FLOPS, bytes_accessed=8 << 20, transcendentals=0),
    )(where, tiles, coupling, inverses)


def call(kernel, out_shape, where, *arrays, scratch=()):
    return pl.pallas_call(
        kernel,
        out_shape=jax.ShapeDtypeStruct(out_shape, jnp.float32),
        in_specs=[pl.BlockSpec(memory_space=pltpu.SMEM)] + [pl.BlockSpec(memory_space=pltpu.VMEM)] * len(arrays),
        scratch_shapes=scratch,
        compiler_params=PARAMS,
        cost_estimate=pl.CostEstimate(flops=3 << 26, bytes_accessed=1 << 20, transcendentals=0),
    )(where, *arrays)


def product(rows, where, index, core, high, low):
    at = (slice(None), where[index], core)
    columns = high.shape[-1]
    return three_passes(rows, high[at].reshape(-1, columns), low[at].reshape(-1, columns))


def first_kernel(where, rows, high, low, out):
    out[...] = product(rows[...], where, 0, where[4], high, low)


def middle_kernel(where, both, up, down, away, sofar, high, low, rhs, solve, out, total):
    share_rows = rhs.shape[0]
    core = where[4]
    total[...] = -sofar[...] - product(both[1 - core], where, 0, 1 - core, high, low)
    for index, rows in enumerate((up, down, away)):
        total[...] -= product(rows[...], where, index + 1, core, high, low)
    at = pl.ds(pl.multiple_of(where[5] * share_rows, share_rows), share_rows)
    total[at, :] += rhs[...]
    out[...] = plain_product(solve[...], total[...])


def last_kernel(where, rows, sofar, high, low, solve, out):
    depth = rows.shape[0] // 3
    other = 1 - where[4]
    update = product(rows[0:depth, :], where, 1, other, high, low)
    update += product(rows[depth : 2 * depth, :], where, 2, other, high, low)
    update += product(rows[2 * depth :, :], where, 3, other, high, low)
    out[...] = (sofar[...] - plain_product(solve[...], update)).reshape(out.shape)


def body(panel, solved, window_rhs, coupling, inverses):
    share_rows, columns = window_rhs.shape
    panel_rows, panel_columns = panel.shape
    grid_columns = lax.axis_size("pcol")
    chips = grid_columns // 2
    far = chips // STRIDE
    row_index = lax.axis_index("prow")
    column_index = lax.axis_index("pcol")
    place = (column_index // 2) % STRIDE
    tiles = solved.reshape(far, STRIDE, 2, panel_rows, columns)
    tiles, coupling, inverses = (
        pltpu.with_memory_space_constraint(array, pltpu.HBM) for array in (tiles, coupling, inverses)
    )

    def shifted(array, up, down):
        pairs = [(2 * z + c, 2 * ((z + (up, down)[c]) % chips) + c) for z in range(chips) for c in range(2)]
        return lax.ppermute(array, "pcol", pairs)

    def swapped(array):
        return lax.ppermute(array, "pcol", [(i, i ^ 1) for i in range(grid_columns)])

    groups = [[2 * (STRIDE * h + l) + c for h in range(far)] for l in range(STRIDE) for c in range(2)]
    own = lax.all_gather(panel, "pcol", axis=0, axis_index_groups=groups, tiled=True)
    first = shifted(own, 1, -1)
    second = shifted(own, -1, 1)
    away = shifted(own, 2, -2)
    core = column_index % 2
    below, above = (place + STRIDE - 1) % STRIDE, (place + 1) % STRIDE
    firsts = [jnp.where(core == 0, below, above), jnp.where(core == 0, above, below)]
    where = jnp.stack([place, *firsts, (place + 2) % STRIDE, core, row_index]).astype(jnp.int32)
    own, where = lax.optimization_barrier((own, where))
    high, low, solve = split(where, tiles, coupling, inverses)
    own, solve = lax.optimization_barrier((own, solve))
    chip = [[2 * z, 2 * z + 1] for z in range(chips)]
    both = lax.all_gather(own, "pcol", axis=0, axis_index_groups=chip)
    shape = (panel_columns, columns)
    sofar = call(first_kernel, shape, where, own, high, low)
    first, second, away, both, sofar = lax.optimization_barrier((first, second, away, both, sofar))
    other = swapped(jnp.concatenate([second, first, away]))
    sofar = call(
        middle_kernel, shape, where, both, first, second, away, sofar, high, low, window_rhs, solve,
        scratch=[pltpu.VMEM(shape, jnp.float32)],
    )
    parts_shape = (shape[0] // share_rows, share_rows, columns)
    parts = call(last_kernel, parts_shape, where, other, sofar, high, low, solve)
    return jnp.sum(lax.all_to_all(parts, "prow", 0, 0), axis=0)


def solution(mesh):
    placed = (P(("prow", "pcol"), None), P("prow", "pcol"), P("prow", "pcol"), P(), P())
    return jax.shard_map(
        body, mesh=mesh, in_specs=placed, out_specs=P("prow", "pcol"), check_vma=False
    )
```

time: 65.9 us -> 65.3 us (level)
  blocking collectives: 38.9 us -> 44 us
  waiting for transfers between devices: 2.84 us -> 0.21 us
  starting transfers between devices: 14.8 us -> 12.4 us
  Pallas kernels: 8.09 us -> 7.42 us
    all_gather x0 -> x1, blocking collectives: none -> 5.14 us  [body(): both = lax.all_gather(own, 'pcol', axis=0, axis_index_groups=chip)]
    ppermute x1, starting transfers between devices: 5.63 us -> 3.22 us  [swapped(): lax.ppermute(array, 'pcol', [(i, i ^ 1) for i in range(grid_columns)])]
    ppermute x3, waiting for transfers between devices: 2.11 us -> 0.01 us  [shifted(): return lax.ppermute(array, 'pcol', pairs)]
    pallas_call x1, Pallas kernels: 4.92 us -> 3.38 us  [split(): pl.pallas_call(split_kernel, out_shape=[half, half, jax.ShapeDtypeStruct(...]
    pallas_call x2 -> x3, Pallas kernels: 3.17 us -> 4.04 us  [call(): pl.pallas_call(kernel, out_shape=jax.ShapeDtypeStruct(out_shape, jnp.floa...]
  transfers between devices with their start and end apart: 4 -> 4, of which waited for: 3 -> 1; matrix products, arithmetic and copies ran while one was open for 0% -> 0% of each run, Pallas kernels for 10% -> 9%
where the time goes in v6:
time: 65.3 us; the launch traced here: 65 us
  blocking collectives  44 us (67%)
  starting transfers between devices  12.4 us (19%)
  Pallas kernels  7.42 us (11%)
  other arithmetic  0.67 us (1%)
    all_gather x1, blocking collectives, body(): lax.all_gather(panel, 'pcol', axis=0, axis_index_groups=groups, tiled=True)  25.5 us
    all_to_all x1, blocking collectives, body(): return jnp.sum(lax.all_to_all(parts, 'prow', 0, 0), axis=0)  13.4 us
    ppermute x3, starting transfers between devices, shifted(): return lax.ppermute(array, 'pcol', pairs)  9.21 us
    all_gather x1, blocking collectives, body(): both = lax.all_gather(own, 'pcol', axis=0, axis_index_groups=chip)  5.14 us
    pallas_call x3, Pallas kernels, call(): pl.pallas_call(kernel, out_shape=jax.ShapeDtypeStruct(out_shape, jnp.floa...  4.04 us
    pallas_call x1, Pallas kernels, split(): pl.pallas_call(split_kernel, out_shape=[half, half, jax.ShapeDtypeStruct(...  3.38 us
    ppermute x1, starting transfers between devices, swapped(): lax.ppermute(array, 'pcol', [(i, i ^ 1) for i in range(grid_columns)])  3.22 us
  transfers between devices with their start and end apart: 4, of which 1 were waited for; matrix products, arithmetic and copies ran while one was open for 0% of the time, Pallas kernels for 9%

profile of v6, /device:TPU:1, one launch (start us, length us, event | category | flops | bytes accessed | tf_op | source)
XLA Modules:
  0.0 65.0 jit_solution(1526789643204524164)
XLA Ops:
  0.0 25.5 %all_gather.9.rows = f32[512,128]{1,0:T(8,128)S(1)} all-gather(f32[128,128]{1,0:T(8,128)} %param.5), channel_id=1, replica_groups={{0,8,16,24},{1,9,17,25},{2,10,18,26},{3,11,19,27},{4,12,20,28},{5,13,21..., dimensions={0}, use_global_device_ids=true | all-gather | bytes 327680 | tf_op jit(solution)/shard_map/all_gather | solution.py:128
  25.5 2.7 %collective-permute-start.2 = (f32[512,128]{1,0:T(8,128)S(1)}, f32[512,128]{1,0:T(8,128)S(1)}, u32[]{:S(2)}, u32[]{:S(2)}) collective-permute-start(f32[512,128]{1,0:T(8,128)S(1)} %all_gather.9.rows), channel_id=1, source_target_pairs={{0,4},{1,29},{2,6},{3,31},{4,8},{5,1},{6,10},{7,3},{8,12},{9,5},{1... | collective-permute-start | bytes 786440 | tf_op jit(solution)/shard_map/ppermute | solution.py:122
  28.2 3.7 %collective-permute-start.1 = (f32[512,128]{1,0:T(8,128)S(1)}, f32[512,128]{1,0:T(8,128)S(1)}, u32[]{:S(2)}, u32[]{:S(2)}) collective-permute-start(f32[512,128]{1,0:T(8,128)S(1)} %all_gather.9.rows), channel_id=1, source_target_pairs={{0,30},{1,3},{2,0},{3,5},{4,2},{5,7},{6,4},{7,9},{8,6},{9,11},{10,... | collective-permute-start | bytes 786440 | tf_op jit(solution)/shard_map/ppermute | solution.py:122
  31.8 2.8 %collective-permute-start = (f32[512,128]{1,0:T(8,128)S(1)}, f32[512,128]{1,0:T(8,128)S(1)}, u32[]{:S(2)}, u32[]{:S(2)}) collective-permute-start(f32[512,128]{1,0:T(8,128)S(1)} %all_gather.9.rows), channel_id=1, source_target_pairs={{0,2},{1,31},{2,4},{3,1},{4,6},{5,3},{6,8},{7,5},{8,10},{9,7},{10,... | collective-permute-start | bytes 786440 | tf_op jit(solution)/shard_map/ppermute | solution.py:122
  34.8 0.1 stack.27.where
  34.9 3.4 %shard_map.55 = (bf16[4,4,2,128,256]{4,3,2,1,0:T(8,128)(2,1)S(1)}, bf16[4,4,2,128,256]{4,3,2,1,0:T(8,128)(2,1)S(1)}, f32[128,128]{1,0:T(8,128)S(1)}) custom-call(s32[6]{0:T(128)S(1)} %stack.27.where, f32[4,4,2,128,256]{4,3,2,1,0:T(8,128)} %bitcast.9, f32[64,64]{1,0:T(8,128)} %coupling.1, f32[2,64,64]{2,1,0:T(8,128)} %inverses.1), custom_call_target="tpu_custom_call" | custom-call | flops 10000000000 | bytes 8388608 | tf_op jit(solution)/shard_map/pallas_call | solution.py:54
  38.2 0.9 %shard_map.56.sofar = f32[128,256]{1,0:T(8,128)S(1)} custom-call(s32[6]{0:T(128)S(1)} %stack.27.where, f32[512,128]{1,0:T(8,128)S(1)} %all_gather.9.rows, bf16[4,4,2,128,256]{4,3,2,1,0:T(8,128)(2,1)S(1)} %get-tuple-element.21.high, bf16[4,4,2,128,256]{4,3,2,1,0:T(8,128)(2,1)S(1)} %get-tuple-element.22.low), custom_call_target="tpu_custom_call" | custom-call | flops 201326592 | bytes 1048576 | tf_op jit(solution)/shard_map/pallas_call | solution.py:66
  39.1 0.0 copy-start
  39.2 5.1 %all-gather = f32[1024,128]{1,0:T(8,128)S(1)} all-gather(f32[512,128]{1,0:T(8,128)S(1)} %all_gather.9.rows), channel_id=2, replica_groups={{0,1},{2,3},{4,5},{6,7},{8,9},{10,11},{12,13},{14,15},{16,17},{18,19},{..., dimensions={0}, use_global_device_ids=true | all-gather | bytes 786432 | tf_op jit(solution)/shard_map/all_gather | solution.py:140
  44.3 0.0 collective-permute-done.2.away
  44.3 0.0 collective-permute-done.1.down
  44.3 0.0 collective-permute-done.up
  44.3 0.1 pad_maximum_fusion
  44.4 3.2 %collective-permute-start.3 = (f32[1536,128]{1,0:T(8,128)S(1)}, f32[1536,128]{1,0:T(8,128)S(1)}, u32[]{:S(2)}, u32[]{:S(2)}) collective-permute-start(f32[1536,128]{1,0:T(8,128)S(1)} %pad_maximum_fusion), channel_id=1, source_target_pairs={{0,1},{1,0},{2,3},{3,2},{4,5},{5,4},{6,7},{7,6},{8,9},{9,8},{10,11... | collective-permute-start | bytes 2359304 | tf_op jit(solution)/shard_map/ppermute | solution.py:125
  47.6 0.0 copy-done
  47.6 1.7 %shard_map.57.sofar = f32[128,256]{1,0:T(8,128)S(1)} custom-call(s32[6]{0:T(128)S(1)} %stack.27.where, f32[2,512,128]{2,1,0:T(8,128)S(1)} %bitcast.8, f32[512,128]{1,0:T(8,128)S(1)} %collective-permute-done.up, f32[512,128]{1,0:T(8,128)S(1)} %collective-permute-done.1.down, f32[512,128]{1,0:T(8,128)S(1)} %collective-permute-done.2.away, ...), custom_call_target="tpu_custom_call" | custom-call | flops 201326592 | bytes 1048576 | tf_op jit(solution)/shard_map/pallas_call | solution.py:66
  49.3 0.2 collective-permute-done.3.rows
  49.5 1.5 %shard_map.58 = f32[16,8,256]{2,1,0:T(8,128)S(1)} custom-call(s32[6]{0:T(128)S(1)} %stack.27.where, f32[1536,128]{1,0:T(8,128)S(1)} %collective-permute-done.3.rows, f32[128,256]{1,0:T(8,128)S(1)} %shard_map.57.sofar, bf16[4,4,2,128,256]{4,3,2,1,0:T(8,128)(2,1)S(1)} %get-tuple-element.21.high, bf16[4,4,2,128,256]{4,3,2,1,0:T(8,128)(2,1)S(1)} %get-tuple-element.22.low, ...), custom_call_target="tpu_custom_call" | custom-call | flops 201326592 | bytes 1048576 | tf_op jit(solution)/shard_map/pallas_call | solution.py:66
  51.0 13.4 %all_to_all.5 = f32[16,8,256]{2,1,0:T(8,128)S(1)} all-to-all(f32[16,8,256]{2,1,0:T(8,128)S(1)} %shard_map.58), channel_id=1, replica_groups=mesh['prow'=16,'pcol'=32] {'prow'}, dimensions={0} | all-to-all | bytes 262144 | tf_op jit(solution)/shard_map/all_to_all | solution.py:151
  64.4 0.6 reduce_sum.9
Async XLA Ops:
  25.5 18.8 %collective-permute-start.2 = (f32[512,128]{1,0:T(8,128)S(1)}, f32[512,128]{1,0:T(8,128)S(1)}, u32[]{:S(2)}, u32[]{:S(2)}) collective-permute-start(f32[512,128]{1,0:T(8,128)S(1)} %all_gather.9.rows), channel_id=1, source_target_pairs={{0,4},{1,29},{2,6},{3,31},{4,8},{5,1},{6,10},{7,3},{8,12},{9,5},{1... | collective-permute-start | bytes 786440 | tf_op jit(solution)/shard_map/ppermute | solution.py:122
  28.2 16.1 %collective-permute-start.1 = (f32[512,128]{1,0:T(8,128)S(1)}, f32[512,128]{1,0:T(8,128)S(1)}, u32[]{:S(2)}, u32[]{:S(2)}) collective-permute-start(f32[512,128]{1,0:T(8,128)S(1)} %all_gather.9.rows), channel_id=1, source_target_pairs={{0,30},{1,3},{2,0},{3,5},{4,2},{5,7},{6,4},{7,9},{8,6},{9,11},{10,... | collective-permute-start | bytes 786440 | tf_op jit(solution)/shard_map/ppermute | solution.py:122
  31.8 12.5 %collective-permute-start = (f32[512,128]{1,0:T(8,128)S(1)}, f32[512,128]{1,0:T(8,128)S(1)}, u32[]{:S(2)}, u32[]{:S(2)}) collective-permute-start(f32[512,128]{1,0:T(8,128)S(1)} %all_gather.9.rows), channel_id=1, source_target_pairs={{0,2},{1,31},{2,4},{3,1},{4,6},{5,3},{6,8},{7,5},{8,10},{9,7},{10,... | collective-permute-start | bytes 786440 | tf_op jit(solution)/shard_map/ppermute | solution.py:122
  39.1 8.5 %copy-start = (f32[8,256]{1,0:T(8,128)S(1)}, f32[8,256]{1,0:T(8,128)}, u32[]{:S(2)}) copy-start(f32[8,256]{1,0:T(8,128)} %rhs.1) | copy-start | bytes 24580
  44.4 5.1 %collective-permute-start.3 = (f32[1536,128]{1,0:T(8,128)S(1)}, f32[1536,128]{1,0:T(8,128)S(1)}, u32[]{:S(2)}, u32[]{:S(2)}) collective-permute-start(f32[1536,128]{1,0:T(8,128)S(1)} %pad_maximum_fusion), channel_id=1, source_target_pairs={{0,1},{1,0},{2,3},{3,2},{4,5},{5,4},{6,7},{7,6},{8,9},{9,8},{10,11... | collective-permute-start | bytes 2359304 | tf_op jit(solution)/shard_map/ppermute | solution.py:125

commit v7 on v6

--- a/solution.py
+++ b/solution.py
@@ -21,9 +21,9 @@
 
 def three_passes(rows, right_high, right_low):
     left_high, left_low = halves(rows.T)
-    total = jnp.dot(left_high, right_high, preferred_element_type=jnp.float32)
-    total += jnp.dot(left_high, right_low, preferred_element_type=jnp.float32)
-    return total + jnp.dot(left_low, right_high, preferred_element_type=jnp.float32)
+    both = jnp.dot(jnp.concatenate([left_high, left_low]), right_high, preferred_element_type=jnp.float32)
+    count = left_high.shape[0]
+    return both[:count] + both[count:] + jnp.dot(left_high, right_low, preferred_element_type=jnp.float32)
 
 
 def split_kernel(where, tiles, coupling, inverses, high, low, solve, held, sems):

time: 65.3 us -> 65.3 us (level)
  no operation moved by 1% of the time
where the time goes in v7:
time: 65.3 us; the launch traced here: 65 us
  blocking collectives  44 us (67%)
  starting transfers between devices  12.4 us (19%)
  Pallas kernels  7.4 us (11%)
  other arithmetic  0.67 us (1%)
    all_gather x1, blocking collectives, body(): lax.all_gather(panel, 'pcol', axis=0, axis_index_groups=groups, tiled=True)  25.5 us
    all_to_all x1, blocking collectives, body(): return jnp.sum(lax.all_to_all(parts, 'prow', 0, 0), axis=0)  13.4 us
    ppermute x3, starting transfers between devices, shifted(): return lax.ppermute(array, 'pcol', pairs)  9.21 us
    all_gather x1, blocking collectives, body(): both = lax.all_gather(own, 'pcol', axis=0, axis_index_groups=chip)  5.14 us
    pallas_call x3, Pallas kernels, call(): pl.pallas_call(kernel, out_shape=jax.ShapeDtypeStruct(out_shape, jnp.floa...  4.01 us
    pallas_call x1, Pallas kernels, split(): pl.pallas_call(split_kernel, out_shape=[half, half, jax.ShapeDtypeStruct(...  3.38 us
    ppermute x1, starting transfers between devices, swapped(): lax.ppermute(array, 'pcol', [(i, i ^ 1) for i in range(grid_columns)])  3.23 us
  transfers between devices with their start and end apart: 4, of which 1 were waited for; matrix products, arithmetic and copies ran while one was open for 0% of the time, Pallas kernels for 9%

profile of v7, /device:TPU:1, one launch (start us, length us, event | category | flops | bytes accessed | tf_op | source)
XLA Modules:
  0.0 65.0 jit_solution(13444086584593254352)
XLA Ops:
  0.0 25.5 %all_gather.9.rows = f32[512,128]{1,0:T(8,128)S(1)} all-gather(f32[128,128]{1,0:T(8,128)} %param.5), channel_id=1, replica_groups={{0,8,16,24},{1,9,17,25},{2,10,18,26},{3,11,19,27},{4,12,20,28},{5,13,21..., dimensions={0}, use_global_device_ids=true | all-gather | bytes 327680 | tf_op jit(solution)/shard_map/all_gather | solution.py:128
  25.5 2.7 %collective-permute-start.2 = (f32[512,128]{1,0:T(8,128)S(1)}, f32[512,128]{1,0:T(8,128)S(1)}, u32[]{:S(2)}, u32[]{:S(2)}) collective-permute-start(f32[512,128]{1,0:T(8,128)S(1)} %all_gather.9.rows), channel_id=1, source_target_pairs={{0,4},{1,29},{2,6},{3,31},{4,8},{5,1},{6,10},{7,3},{8,12},{9,5},{1... | collective-permute-start | bytes 786440 | tf_op jit(solution)/shard_map/ppermute | solution.py:122
  28.2 3.7 %collective-permute-start.1 = (f32[512,128]{1,0:T(8,128)S(1)}, f32[512,128]{1,0:T(8,128)S(1)}, u32[]{:S(2)}, u32[]{:S(2)}) collective-permute-start(f32[512,128]{1,0:T(8,128)S(1)} %all_gather.9.rows), channel_id=1, source_target_pairs={{0,30},{1,3},{2,0},{3,5},{4,2},{5,7},{6,4},{7,9},{8,6},{9,11},{10,... | collective-permute-start | bytes 786440 | tf_op jit(solution)/shard_map/ppermute | solution.py:122
  31.8 2.8 %collective-permute-start = (f32[512,128]{1,0:T(8,128)S(1)}, f32[512,128]{1,0:T(8,128)S(1)}, u32[]{:S(2)}, u32[]{:S(2)}) collective-permute-start(f32[512,128]{1,0:T(8,128)S(1)} %all_gather.9.rows), channel_id=1, source_target_pairs={{0,2},{1,31},{2,4},{3,1},{4,6},{5,3},{6,8},{7,5},{8,10},{9,7},{10,... | collective-permute-start | bytes 786440 | tf_op jit(solution)/shard_map/ppermute | solution.py:122
  34.8 0.1 stack.27.where
  34.9 3.4 %shard_map.55 = (bf16[4,4,2,128,256]{4,3,2,1,0:T(8,128)(2,1)S(1)}, bf16[4,4,2,128,256]{4,3,2,1,0:T(8,128)(2,1)S(1)}, f32[128,128]{1,0:T(8,128)S(1)}) custom-call(s32[6]{0:T(128)S(1)} %stack.27.where, f32[4,4,2,128,256]{4,3,2,1,0:T(8,128)} %bitcast.9, f32[64,64]{1,0:T(8,128)} %coupling.1, f32[2,64,64]{2,1,0:T(8,128)} %inverses.1), custom_call_target="tpu_custom_call" | custom-call | flops 10000000000 | bytes 8388608 | tf_op jit(solution)/shard_map/pallas_call | solution.py:54
  38.2 0.9 %shard_map.56.sofar = f32[128,256]{1,0:T(8,128)S(1)} custom-call(s32[6]{0:T(128)S(1)} %stack.27.where, f32[512,128]{1,0:T(8,128)S(1)} %all_gather.9.rows, bf16[4,4,2,128,256]{4,3,2,1,0:T(8,128)(2,1)S(1)} %get-tuple-element.21.high, bf16[4,4,2,128,256]{4,3,2,1,0:T(8,128)(2,1)S(1)} %get-tuple-element.22.low), custom_call_target="tpu_custom_call" | custom-call | flops 201326592 | bytes 1048576 | tf_op jit(solution)/shard_map/pallas_call | solution.py:66
  39.1 0.0 copy-start
  39.1 5.1 %all-gather = f32[1024,128]{1,0:T(8,128)S(1)} all-gather(f32[512,128]{1,0:T(8,128)S(1)} %all_gather.9.rows), channel_id=2, replica_groups={{0,1},{2,3},{4,5},{6,7},{8,9},{10,11},{12,13},{14,15},{16,17},{18,19},{..., dimensions={0}, use_global_device_ids=true | all-gather | bytes 786432 | tf_op jit(solution)/shard_map/all_gather | solution.py:140
  44.3 0.0 collective-permute-done.2.away
  44.3 0.0 collective-permute-done.1.down
  44.3 0.0 collective-permute-done.up
  44.3 0.1 pad_maximum_fusion
  44.4 3.2 %collective-permute-start.3 = (f32[1536,128]{1,0:T(8,128)S(1)}, f32[1536,128]{1,0:T(8,128)S(1)}, u32[]{:S(2)}, u32[]{:S(2)}) collective-permute-start(f32[1536,128]{1,0:T(8,128)S(1)} %pad_maximum_fusion), channel_id=1, source_target_pairs={{0,1},{1,0},{2,3},{3,2},{4,5},{5,4},{6,7},{7,6},{8,9},{9,8},{10,11... | collective-permute-start | bytes 2359304 | tf_op jit(solution)/shard_map/ppermute | solution.py:125
  47.6 0.0 copy-done
  47.6 1.6 %shard_map.57.sofar = f32[128,256]{1,0:T(8,128)S(1)} custom-call(s32[6]{0:T(128)S(1)} %stack.27.where, f32[2,512,128]{2,1,0:T(8,128)S(1)} %bitcast.8, f32[512,128]{1,0:T(8,128)S(1)} %collective-permute-done.up, f32[512,128]{1,0:T(8,128)S(1)} %collective-permute-done.1.down, f32[512,128]{1,0:T(8,128)S(1)} %collective-permute-done.2.away, ...), custom_call_target="tpu_custom_call" | custom-call | flops 201326592 | bytes 1048576 | tf_op jit(solution)/shard_map/pallas_call | solution.py:66
  49.3 0.2 collective-permute-done.3.rows
  49.5 1.5 %shard_map.58 = f32[16,8,256]{2,1,0:T(8,128)S(1)} custom-call(s32[6]{0:T(128)S(1)} %stack.27.where, f32[1536,128]{1,0:T(8,128)S(1)} %collective-permute-done.3.rows, f32[128,256]{1,0:T(8,128)S(1)} %shard_map.57.sofar, bf16[4,4,2,128,256]{4,3,2,1,0:T(8,128)(2,1)S(1)} %get-tuple-element.21.high, bf16[4,4,2,128,256]{4,3,2,1,0:T(8,128)(2,1)S(1)} %get-tuple-element.22.low, ...), custom_call_target="tpu_custom_call" | custom-call | flops 201326592 | bytes 1048576 | tf_op jit(solution)/shard_map/pallas_call | solution.py:66
  51.0 13.4 %all_to_all.5 = f32[16,8,256]{2,1,0:T(8,128)S(1)} all-to-all(f32[16,8,256]{2,1,0:T(8,128)S(1)} %shard_map.58), channel_id=1, replica_groups=mesh['prow'=16,'pcol'=32] {'prow'}, dimensions={0} | all-to-all | bytes 262144 | tf_op jit(solution)/shard_map/all_to_all | solution.py:151
  64.4 0.6 reduce_sum.9
Async XLA Ops:
  25.5 18.8 %collective-permute-start.2 = (f32[512,128]{1,0:T(8,128)S(1)}, f32[512,128]{1,0:T(8,128)S(1)}, u32[]{:S(2)}, u32[]{:S(2)}) collective-permute-start(f32[512,128]{1,0:T(8,128)S(1)} %all_gather.9.rows), channel_id=1, source_target_pairs={{0,4},{1,29},{2,6},{3,31},{4,8},{5,1},{6,10},{7,3},{8,12},{9,5},{1... | collective-permute-start | bytes 786440 | tf_op jit(solution)/shard_map/ppermute | solution.py:122
  28.2 16.1 %collective-permute-start.1 = (f32[512,128]{1,0:T(8,128)S(1)}, f32[512,128]{1,0:T(8,128)S(1)}, u32[]{:S(2)}, u32[]{:S(2)}) collective-permute-start(f32[512,128]{1,0:T(8,128)S(1)} %all_gather.9.rows), channel_id=1, source_target_pairs={{0,30},{1,3},{2,0},{3,5},{4,2},{5,7},{6,4},{7,9},{8,6},{9,11},{10,... | collective-permute-start | bytes 786440 | tf_op jit(solution)/shard_map/ppermute | solution.py:122
  31.8 12.4 %collective-permute-start = (f32[512,128]{1,0:T(8,128)S(1)}, f32[512,128]{1,0:T(8,128)S(1)}, u32[]{:S(2)}, u32[]{:S(2)}) collective-permute-start(f32[512,128]{1,0:T(8,128)S(1)} %all_gather.9.rows), channel_id=1, source_target_pairs={{0,2},{1,31},{2,4},{3,1},{4,6},{5,3},{6,8},{7,5},{8,10},{9,7},{10,... | collective-permute-start | bytes 786440 | tf_op jit(solution)/shard_map/ppermute | solution.py:122
  39.1 8.5 %copy-start = (f32[8,256]{1,0:T(8,128)S(1)}, f32[8,256]{1,0:T(8,128)}, u32[]{:S(2)}) copy-start(f32[8,256]{1,0:T(8,128)} %rhs.1) | copy-start | bytes 24580
  44.4 5.1 %collective-permute-start.3 = (f32[1536,128]{1,0:T(8,128)S(1)}, f32[1536,128]{1,0:T(8,128)S(1)}, u32[]{:S(2)}, u32[]{:S(2)}) collective-permute-start(f32[1536,128]{1,0:T(8,128)S(1)} %pad_maximum_fusion), channel_id=1, source_target_pairs={{0,1},{1,0},{2,3},{3,2},{4,5},{5,4},{6,7},{7,6},{8,9},{9,8},{10,11... | collective-permute-start | bytes 2359304 | tf_op jit(solution)/shard_map/ppermute | solution.py:125

commit v8 on v7

--- a/solution.py
+++ b/solution.py
@@ -21,6 +21,14 @@
 
 def three_passes(rows, right_high, right_low):
     left_high, left_low = halves(rows.T)
+    both = jnp.dot(jnp.concatenate([left_high, left_low]), right_high, preferred_element_type=jnp.float32)
+    count = left_high.shape[0]
+    return both[:count] + both[count:] + jnp.dot(left_high, right_low, preferred_element_type=jnp.float32)
+
+
+def solved_product(solve, array):
+    left_high, left_low = halves(solve)
+    right_high, right_low = halves(array)
     both = jnp.dot(jnp.concatenate([left_high, left_low]), right_high, preferred_element_type=jnp.float32)
     count = left_high.shape[0]
     return both[:count] + both[count:] + jnp.dot(left_high, right_low, preferred_element_type=jnp.float32)
@@ -91,7 +99,7 @@
         total[...] -= product(rows[...], where, index + 1, core, high, low)
     at = pl.ds(pl.multiple_of(where[5] * share_rows, share_rows), share_rows)
     total[at, :] += rhs[...]
-    out[...] = plain_product(solve[...], total[...])
+    out[...] = solved_product(solve[...], total[...])
 
 
 def last_kernel(where, rows, sofar, high, low, solve, out):
@@ -100,7 +108,7 @@
     update = product(rows[0:depth, :], where, 1, other, high, low)
     update += product(rows[depth : 2 * depth, :], where, 2, other, high, low)
     update += product(rows[2 * depth :, :], where, 3, other, high, low)
-    out[...] = (sofar[...] - plain_product(solve[...], update)).reshape(out.shape)
+    out[...] = (sofar[...] - solved_product(solve[...], update)).reshape(out.shape)
 
 
 def body(panel, solved, window_rhs, coupling, inverses):

time: 65.3 us -> 65.2 us (level)
  no operation moved by 1% of the time
where the time goes in v8:
time: 65.2 us; the launch traced here: 64.8 us
  blocking collectives  44 us (67%)
  starting transfers between devices  12.4 us (19%)
  Pallas kernels  6.99 us (11%)
  other arithmetic  0.67 us (1%)
    all_gather x1, blocking collectives, body(): lax.all_gather(panel, 'pcol', axis=0, axis_index_groups=groups, tiled=True)  25.5 us
    all_to_all x1, blocking collectives, body(): return jnp.sum(lax.all_to_all(parts, 'prow', 0, 0), axis=0)  13.4 us
    ppermute x3, starting transfers between devices, shifted(): return lax.ppermute(array, 'pcol', pairs)  9.21 us
    all_gather x1, blocking collectives, body(): both = lax.all_gather(own, 'pcol', axis=0, axis_index_groups=chip)  5.14 us
    pallas_call x3, Pallas kernels, call(): pl.pallas_call(kernel, out_shape=jax.ShapeDtypeStruct(out_shape, jnp.floa...  3.61 us
    pallas_call x1, Pallas kernels, split(): pl.pallas_call(split_kernel, out_shape=[half, half, jax.ShapeDtypeStruct(...  3.38 us
    ppermute x1, starting transfers between devices, swapped(): lax.ppermute(array, 'pcol', [(i, i ^ 1) for i in range(grid_columns)])  3.23 us
  transfers between devices with their start and end apart: 4, of which 1 were waited for; matrix products, arithmetic and copies ran while one was open for 0% of the time, Pallas kernels for 9%

profile of v8, /device:TPU:1, one launch (start us, length us, event | category | flops | bytes accessed | tf_op | source)
XLA Modules:
  0.0 64.8 jit_solution(2174753626242974298)
XLA Ops:
  0.0 25.5 %all_gather.9.rows = f32[512,128]{1,0:T(8,128)S(1)} all-gather(f32[128,128]{1,0:T(8,128)} %param.5), channel_id=1, replica_groups={{0,8,16,24},{1,9,17,25},{2,10,18,26},{3,11,19,27},{4,12,20,28},{5,13,21..., dimensions={0}, use_global_device_ids=true | all-gather | bytes 327680 | tf_op jit(solution)/shard_map/all_gather | solution.py:136
  25.5 2.7 %collective-permute-start.2 = (f32[512,128]{1,0:T(8,128)S(1)}, f32[512,128]{1,0:T(8,128)S(1)}, u32[]{:S(2)}, u32[]{:S(2)}) collective-permute-start(f32[512,128]{1,0:T(8,128)S(1)} %all_gather.9.rows), channel_id=1, source_target_pairs={{0,4},{1,29},{2,6},{3,31},{4,8},{5,1},{6,10},{7,3},{8,12},{9,5},{1... | collective-permute-start | bytes 786440 | tf_op jit(solution)/shard_map/ppermute | solution.py:130
  28.2 3.7 %collective-permute-start.1 = (f32[512,128]{1,0:T(8,128)S(1)}, f32[512,128]{1,0:T(8,128)S(1)}, u32[]{:S(2)}, u32[]{:S(2)}) collective-permute-start(f32[512,128]{1,0:T(8,128)S(1)} %all_gather.9.rows), channel_id=1, source_target_pairs={{0,30},{1,3},{2,0},{3,5},{4,2},{5,7},{6,4},{7,9},{8,6},{9,11},{10,... | collective-permute-start | bytes 786440 | tf_op jit(solution)/shard_map/ppermute | solution.py:130
  31.8 2.8 %collective-permute-start = (f32[512,128]{1,0:T(8,128)S(1)}, f32[512,128]{1,0:T(8,128)S(1)}, u32[]{:S(2)}, u32[]{:S(2)}) collective-permute-start(f32[512,128]{1,0:T(8,128)S(1)} %all_gather.9.rows), channel_id=1, source_target_pairs={{0,2},{1,31},{2,4},{3,1},{4,6},{5,3},{6,8},{7,5},{8,10},{9,7},{10,... | collective-permute-start | bytes 786440 | tf_op jit(solution)/shard_map/ppermute | solution.py:130
  34.8 0.1 stack.27.where
  34.9 3.4 %shard_map.55 = (bf16[4,4,2,128,256]{4,3,2,1,0:T(8,128)(2,1)S(1)}, bf16[4,4,2,128,256]{4,3,2,1,0:T(8,128)(2,1)S(1)}, f32[128,128]{1,0:T(8,128)S(1)}) custom-call(s32[6]{0:T(128)S(1)} %stack.27.where, f32[4,4,2,128,256]{4,3,2,1,0:T(8,128)} %bitcast.9, f32[64,64]{1,0:T(8,128)} %coupling.1, f32[2,64,64]{2,1,0:T(8,128)} %inverses.1), custom_call_target="tpu_custom_call" | custom-call | flops 10000000000 | bytes 8388608 | tf_op jit(solution)/shard_map/pallas_call | solution.py:62
  38.2 0.9 %shard_map.56.sofar = f32[128,256]{1,0:T(8,128)S(1)} custom-call(s32[6]{0:T(128)S(1)} %stack.27.where, f32[512,128]{1,0:T(8,128)S(1)} %all_gather.9.rows, bf16[4,4,2,128,256]{4,3,2,1,0:T(8,128)(2,1)S(1)} %get-tuple-element.21.high, bf16[4,4,2,128,256]{4,3,2,1,0:T(8,128)(2,1)S(1)} %get-tuple-element.22.low), custom_call_target="tpu_custom_call" | custom-call | flops 201326592 | bytes 1048576 | tf_op jit(solution)/shard_map/pallas_call | solution.py:74
  39.1 0.0 copy-start
  39.1 5.1 %all-gather = f32[1024,128]{1,0:T(8,128)S(1)} all-gather(f32[512,128]{1,0:T(8,128)S(1)} %all_gather.9.rows), channel_id=2, replica_groups={{0,1},{2,3},{4,5},{6,7},{8,9},{10,11},{12,13},{14,15},{16,17},{18,19},{..., dimensions={0}, use_global_device_ids=true | all-gather | bytes 786432 | tf_op jit(solution)/shard_map/all_gather | solution.py:148
  44.3 0.0 collective-permute-done.2.away
  44.3 0.0 collective-permute-done.1.down
  44.3 0.0 collective-permute-done.up
  44.3 0.1 pad_maximum_fusion
  44.4 3.2 %collective-permute-start.3 = (f32[1536,128]{1,0:T(8,128)S(1)}, f32[1536,128]{1,0:T(8,128)S(1)}, u32[]{:S(2)}, u32[]{:S(2)}) collective-permute-start(f32[1536,128]{1,0:T(8,128)S(1)} %pad_maximum_fusion), channel_id=1, source_target_pairs={{0,1},{1,0},{2,3},{3,2},{4,5},{5,4},{6,7},{7,6},{8,9},{9,8},{10,11... | collective-permute-start | bytes 2359304 | tf_op jit(solution)/shard_map/ppermute | solution.py:133
  47.6 0.0 copy-done
  47.6 1.4 %shard_map.57.sofar = f32[128,256]{1,0:T(8,128)S(1)} custom-call(s32[6]{0:T(128)S(1)} %stack.27.where, f32[2,512,128]{2,1,0:T(8,128)S(1)} %bitcast.8, f32[512,128]{1,0:T(8,128)S(1)} %collective-permute-done.up, f32[512,128]{1,0:T(8,128)S(1)} %collective-permute-done.1.down, f32[512,128]{1,0:T(8,128)S(1)} %collective-permute-done.2.away, ...), custom_call_target="tpu_custom_call" | custom-call | flops 201326592 | bytes 1048576 | tf_op jit(solution)/shard_map/pallas_call | solution.py:74
  49.0 0.5 collective-permute-done.3.rows
  49.5 1.3 %shard_map.58 = f32[16,8,256]{2,1,0:T(8,128)S(1)} custom-call(s32[6]{0:T(128)S(1)} %stack.27.where, f32[1536,128]{1,0:T(8,128)S(1)} %collective-permute-done.3.rows, f32[128,256]{1,0:T(8,128)S(1)} %shard_map.57.sofar, bf16[4,4,2,128,256]{4,3,2,1,0:T(8,128)(2,1)S(1)} %get-tuple-element.21.high, bf16[4,4,2,128,256]{4,3,2,1,0:T(8,128)(2,1)S(1)} %get-tuple-element.22.low, ...), custom_call_target="tpu_custom_call" | custom-call | flops 201326592 | bytes 1048576 | tf_op jit(solution)/shard_map/pallas_call | solution.py:74
  50.8 13.4 %all_to_all.5 = f32[16,8,256]{2,1,0:T(8,128)S(1)} all-to-all(f32[16,8,256]{2,1,0:T(8,128)S(1)} %shard_map.58), channel_id=1, replica_groups=mesh['prow'=16,'pcol'=32] {'prow'}, dimensions={0} | all-to-all | bytes 262144 | tf_op jit(solution)/shard_map/all_to_all | solution.py:159
  64.2 0.6 reduce_sum.9
Async XLA Ops:
  25.5 18.8 %collective-permute-start.2 = (f32[512,128]{1,0:T(8,128)S(1)}, f32[512,128]{1,0:T(8,128)S(1)}, u32[]{:S(2)}, u32[]{:S(2)}) collective-permute-start(f32[512,128]{1,0:T(8,128)S(1)} %all_gather.9.rows), channel_id=1, source_target_pairs={{0,4},{1,29},{2,6},{3,31},{4,8},{5,1},{6,10},{7,3},{8,12},{9,5},{1... | collective-permute-start | bytes 786440 | tf_op jit(solution)/shard_map/ppermute | solution.py:130
  28.2 16.1 %collective-permute-start.1 = (f32[512,128]{1,0:T(8,128)S(1)}, f32[512,128]{1,0:T(8,128)S(1)}, u32[]{:S(2)}, u32[]{:S(2)}) collective-permute-start(f32[512,128]{1,0:T(8,128)S(1)} %all_gather.9.rows), channel_id=1, source_target_pairs={{0,30},{1,3},{2,0},{3,5},{4,2},{5,7},{6,4},{7,9},{8,6},{9,11},{10,... | collective-permute-start | bytes 786440 | tf_op jit(solution)/shard_map/ppermute | solution.py:130
  31.8 12.4 %collective-permute-start = (f32[512,128]{1,0:T(8,128)S(1)}, f32[512,128]{1,0:T(8,128)S(1)}, u32[]{:S(2)}, u32[]{:S(2)}) collective-permute-start(f32[512,128]{1,0:T(8,128)S(1)} %all_gather.9.rows), channel_id=1, source_target_pairs={{0,2},{1,31},{2,4},{3,1},{4,6},{5,3},{6,8},{7,5},{8,10},{9,7},{10,... | collective-permute-start | bytes 786440 | tf_op jit(solution)/shard_map/ppermute | solution.py:130
  39.1 8.5 %copy-start = (f32[8,256]{1,0:T(8,128)S(1)}, f32[8,256]{1,0:T(8,128)}, u32[]{:S(2)}) copy-start(f32[8,256]{1,0:T(8,128)} %rhs.1) | copy-start | bytes 24580
  44.4 5.1 %collective-permute-start.3 = (f32[1536,128]{1,0:T(8,128)S(1)}, f32[1536,128]{1,0:T(8,128)S(1)}, u32[]{:S(2)}, u32[]{:S(2)}) collective-permute-start(f32[1536,128]{1,0:T(8,128)S(1)} %pad_maximum_fusion), channel_id=1, source_target_pairs={{0,1},{1,0},{2,3},{3,2},{4,5},{5,4},{6,7},{7,6},{8,9},{9,8},{10,11... | collective-permute-start | bytes 2359304 | tf_op jit(solution)/shard_map/ppermute | solution.py:133

commit v9 on v8

--- a/solution.py
+++ b/solution.py
@@ -129,18 +129,20 @@
         pairs = [(2 * z + c, 2 * ((z + (up, down)[c]) % chips) + c) for z in range(chips) for c in range(2)]
         return lax.ppermute(array, "pcol", pairs)
 
+    def exchanged(array, odd):
+        pairs = [(2 * z + c, 2 * ((((z + odd) ^ 1) - odd) % chips) + c) for z in range(chips) for c in range(2)]
+        return lax.ppermute(array, "pcol", pairs)
+
     def swapped(array):
         return lax.ppermute(array, "pcol", [(i, i ^ 1) for i in range(grid_columns)])
 
     groups = [[2 * (STRIDE * h + l) + c for h in range(far)] for l in range(STRIDE) for c in range(2)]
     own = lax.all_gather(panel, "pcol", axis=0, axis_index_groups=groups, tiled=True)
-    first = shifted(own, 1, -1)
-    second = shifted(own, -1, 1)
+    first = exchanged(own, 0)
+    second = exchanged(own, 1)
     away = shifted(own, 2, -2)
-    core = column_index % 2
-    below, above = (place + STRIDE - 1) % STRIDE, (place + 1) % STRIDE
-    firsts = [jnp.where(core == 0, below, above), jnp.where(core == 0, above, below)]
-    where = jnp.stack([place, *firsts, (place + 2) % STRIDE, core, row_index]).astype(jnp.int32)
+    places = [place, place ^ 1, place ^ 3, place ^ 2]
+    where = jnp.stack([*places, column_index % 2, row_index]).astype(jnp.int32)
     own, where = lax.optimization_barrier((own, where))
     high, low, solve = split(where, tiles, coupling, inverses)
     own, solve = lax.optimization_barrier((own, solve))
@@ -149,7 +151,7 @@
     shape = (panel_columns, columns)
     sofar = call(first_kernel, shape, where, own, high, low)
     first, second, away, both, sofar = lax.optimization_barrier((first, second, away, both, sofar))
-    other = swapped(jnp.concatenate([second, first, away]))
+    other = swapped(jnp.concatenate([first, second, away]))
     sofar = call(
         middle_kernel, shape, where, both, first, second, away, sofar, high, low, window_rhs, solve,
         scratch=[pltpu.VMEM(shape, jnp.float32)],

time: 65.2 us -> 65.2 us (level)
  blocking collectives: 44 us -> 45.7 us
  starting transfers between devices: 12.4 us -> 10.8 us
    ppermute x3 -> x1, starting transfers between devices: 9.21 us -> 2.72 us  [shifted(): return lax.ppermute(array, 'pcol', pairs)]
    ppermute x0 -> x2, starting transfers between devices: none -> 5.65 us  [exchanged(): return lax.ppermute(array, 'pcol', pairs)]
    all_gather x1, blocking collectives: 5.14 us -> 6.87 us  [body(): both = lax.all_gather(own, 'pcol', axis=0, axis_index_groups=chip)]
    ppermute x1, starting transfers between devices: 3.23 us -> 2.39 us  [swapped(): lax.ppermute(array, 'pcol', [(i, i ^ 1) for i in range(grid_columns)])]
where the time goes in v9:
time: 65.2 us; the launch traced here: 64.8 us
  blocking collectives  45.7 us (70%)
  starting transfers between devices  10.8 us (17%)
  Pallas kernels  7.01 us (11%)
  other arithmetic  0.67 us (1%)
    all_gather x1, blocking collectives, body(): lax.all_gather(panel, 'pcol', axis=0, axis_index_groups=groups, tiled=True)  25.5 us
    all_to_all x1, blocking collectives, body(): return jnp.sum(lax.all_to_all(parts, 'prow', 0, 0), axis=0)  13.4 us
    all_gather x1, blocking collectives, body(): both = lax.all_gather(own, 'pcol', axis=0, axis_index_groups=chip)  6.87 us
    ppermute x2, starting transfers between devices, exchanged(): return lax.ppermute(array, 'pcol', pairs)  5.65 us
    pallas_call x3, Pallas kernels, call(): pl.pallas_call(kernel, out_shape=jax.ShapeDtypeStruct(out_shape, jnp.floa...  3.63 us
    pallas_call x1, Pallas kernels, split(): pl.pallas_call(split_kernel, out_shape=[half, half, jax.ShapeDtypeStruct(...  3.38 us
    ppermute x1, starting transfers between devices, shifted(): return lax.ppermute(array, 'pcol', pairs)  2.72 us
    ppermute x1, starting transfers between devices, swapped(): lax.ppermute(array, 'pcol', [(i, i ^ 1) for i in range(grid_columns)])  2.39 us
  transfers between devices with their start and end apart: 4, of which 1 were waited for; matrix products, arithmetic and copies ran while one was open for 0% of the time, Pallas kernels for 9%

profile of v9, /device:TPU:1, one launch (start us, length us, event | category | flops | bytes accessed | tf_op | source)
XLA Modules:
  0.0 64.8 jit_solution(12340063281414355686)
XLA Ops:
  0.0 25.5 %all_gather.9.rows = f32[512,128]{1,0:T(8,128)S(1)} all-gather(f32[128,128]{1,0:T(8,128)} %param.5), channel_id=1, replica_groups={{0,8,16,24},{1,9,17,25},{2,10,18,26},{3,11,19,27},{4,12,20,28},{5,13,21..., dimensions={0}, use_global_device_ids=true | all-gather | bytes 327680 | tf_op jit(solution)/shard_map/all_gather | solution.py:140
  25.5 2.7 %collective-permute-start.2 = (f32[512,128]{1,0:T(8,128)S(1)}, f32[512,128]{1,0:T(8,128)S(1)}, u32[]{:S(2)}, u32[]{:S(2)}) collective-permute-start(f32[512,128]{1,0:T(8,128)S(1)} %all_gather.9.rows), channel_id=1, source_target_pairs={{0,4},{1,29},{2,6},{3,31},{4,8},{5,1},{6,10},{7,3},{8,12},{9,5},{1... | collective-permute-start | bytes 786440 | tf_op jit(solution)/shard_map/ppermute | solution.py:130
  28.2 2.6 %collective-permute-start.1 = (f32[512,128]{1,0:T(8,128)S(1)}, f32[512,128]{1,0:T(8,128)S(1)}, u32[]{:S(2)}, u32[]{:S(2)}) collective-permute-start(f32[512,128]{1,0:T(8,128)S(1)} %all_gather.9.rows), channel_id=1, source_target_pairs={{0,30},{1,31},{2,4},{3,5},{4,2},{5,3},{6,8},{7,9},{8,6},{9,7},{10,... | collective-permute-start | bytes 786440 | tf_op jit(solution)/shard_map/ppermute | solution.py:134
  30.8 3.0 %collective-permute-start = (f32[512,128]{1,0:T(8,128)S(1)}, f32[512,128]{1,0:T(8,128)S(1)}, u32[]{:S(2)}, u32[]{:S(2)}) collective-permute-start(f32[512,128]{1,0:T(8,128)S(1)} %all_gather.9.rows), channel_id=1, source_target_pairs={{0,2},{1,3},{2,0},{3,1},{4,6},{5,7},{6,4},{7,5},{8,10},{9,11},{10,... | collective-permute-start | bytes 786440 | tf_op jit(solution)/shard_map/ppermute | solution.py:134
  33.9 0.1 stack.27.where
  34.0 3.4 %shard_map.55 = (bf16[4,4,2,128,256]{4,3,2,1,0:T(8,128)(2,1)S(1)}, bf16[4,4,2,128,256]{4,3,2,1,0:T(8,128)(2,1)S(1)}, f32[128,128]{1,0:T(8,128)S(1)}) custom-call(s32[6]{0:T(128)S(1)} %stack.27.where, f32[4,4,2,128,256]{4,3,2,1,0:T(8,128)} %bitcast.9, f32[64,64]{1,0:T(8,128)} %coupling.1, f32[2,64,64]{2,1,0:T(8,128)} %inverses.1), custom_call_target="tpu_custom_call" | custom-call | flops 10000000000 | bytes 8388608 | tf_op jit(solution)/shard_map/pallas_call | solution.py:62
  37.4 0.9 %shard_map.56.sofar = f32[128,256]{1,0:T(8,128)S(1)} custom-call(s32[6]{0:T(128)S(1)} %stack.27.where, f32[512,128]{1,0:T(8,128)S(1)} %all_gather.9.rows, bf16[4,4,2,128,256]{4,3,2,1,0:T(8,128)(2,1)S(1)} %get-tuple-element.21.high, bf16[4,4,2,128,256]{4,3,2,1,0:T(8,128)(2,1)S(1)} %get-tuple-element.22.low), custom_call_target="tpu_custom_call" | custom-call | flops 201326592 | bytes 1048576 | tf_op jit(solution)/shard_map/pallas_call | solution.py:74
  38.2 0.0 copy-start
  38.3 6.9 %all-gather = f32[1024,128]{1,0:T(8,128)S(1)} all-gather(f32[512,128]{1,0:T(8,128)S(1)} %all_gather.9.rows), channel_id=2, replica_groups={{0,1},{2,3},{4,5},{6,7},{8,9},{10,11},{12,13},{14,15},{16,17},{18,19},{..., dimensions={0}, use_global_device_ids=true | all-gather | bytes 786432 | tf_op jit(solution)/shard_map/all_gather | solution.py:150
  45.1 0.0 collective-permute-done.2.away
  45.1 0.0 collective-permute-done.1.down
  45.1 0.0 collective-permute-done.up
  45.1 0.1 pad_maximum_fusion
  45.2 2.4 %collective-permute-start.3 = (f32[1536,128]{1,0:T(8,128)S(1)}, f32[1536,128]{1,0:T(8,128)S(1)}, u32[]{:S(2)}, u32[]{:S(2)}) collective-permute-start(f32[1536,128]{1,0:T(8,128)S(1)} %pad_maximum_fusion), channel_id=1, source_target_pairs={{0,1},{1,0},{2,3},{3,2},{4,5},{5,4},{6,7},{7,6},{8,9},{9,8},{10,11... | collective-permute-start | bytes 2359304 | tf_op jit(solution)/shard_map/ppermute | solution.py:137
  47.6 0.0 copy-done
  47.6 1.4 %shard_map.57.sofar = f32[128,256]{1,0:T(8,128)S(1)} custom-call(s32[6]{0:T(128)S(1)} %stack.27.where, f32[2,512,128]{2,1,0:T(8,128)S(1)} %bitcast.8, f32[512,128]{1,0:T(8,128)S(1)} %collective-permute-done.up, f32[512,128]{1,0:T(8,128)S(1)} %collective-permute-done.1.down, f32[512,128]{1,0:T(8,128)S(1)} %collective-permute-done.2.away, ...), custom_call_target="tpu_custom_call" | custom-call | flops 201326592 | bytes 1048576 | tf_op jit(solution)/shard_map/pallas_call | solution.py:74
  49.0 0.5 collective-permute-done.3.rows
  49.5 1.3 %shard_map.58 = f32[16,8,256]{2,1,0:T(8,128)S(1)} custom-call(s32[6]{0:T(128)S(1)} %stack.27.where, f32[1536,128]{1,0:T(8,128)S(1)} %collective-permute-done.3.rows, f32[128,256]{1,0:T(8,128)S(1)} %shard_map.57.sofar, bf16[4,4,2,128,256]{4,3,2,1,0:T(8,128)(2,1)S(1)} %get-tuple-element.21.high, bf16[4,4,2,128,256]{4,3,2,1,0:T(8,128)(2,1)S(1)} %get-tuple-element.22.low, ...), custom_call_target="tpu_custom_call" | custom-call | flops 201326592 | bytes 1048576 | tf_op jit(solution)/shard_map/pallas_call | solution.py:74
  50.8 13.4 %all_to_all.5 = f32[16,8,256]{2,1,0:T(8,128)S(1)} all-to-all(f32[16,8,256]{2,1,0:T(8,128)S(1)} %shard_map.58), channel_id=1, replica_groups=mesh['prow'=16,'pcol'=32] {'prow'}, dimensions={0} | all-to-all | bytes 262144 | tf_op jit(solution)/shard_map/all_to_all | solution.py:161
  64.2 0.6 reduce_sum.9
Async XLA Ops:
  25.5 19.7 %collective-permute-start.2 = (f32[512,128]{1,0:T(8,128)S(1)}, f32[512,128]{1,0:T(8,128)S(1)}, u32[]{:S(2)}, u32[]{:S(2)}) collective-permute-start(f32[512,128]{1,0:T(8,128)S(1)} %all_gather.9.rows), channel_id=1, source_target_pairs={{0,4},{1,29},{2,6},{3,31},{4,8},{5,1},{6,10},{7,3},{8,12},{9,5},{1... | collective-permute-start | bytes 786440 | tf_op jit(solution)/shard_map/ppermute | solution.py:130
  28.2 17.0 %collective-permute-start.1 = (f32[512,128]{1,0:T(8,128)S(1)}, f32[512,128]{1,0:T(8,128)S(1)}, u32[]{:S(2)}, u32[]{:S(2)}) collective-permute-start(f32[512,128]{1,0:T(8,128)S(1)} %all_gather.9.rows), channel_id=1, source_target_pairs={{0,30},{1,31},{2,4},{3,5},{4,2},{5,3},{6,8},{7,9},{8,6},{9,7},{10,... | collective-permute-start | bytes 786440 | tf_op jit(solution)/shard_map/ppermute | solution.py:134
  30.8 14.3 %collective-permute-start = (f32[512,128]{1,0:T(8,128)S(1)}, f32[512,128]{1,0:T(8,128)S(1)}, u32[]{:S(2)}, u32[]{:S(2)}) collective-permute-start(f32[512,128]{1,0:T(8,128)S(1)} %all_gather.9.rows), channel_id=1, source_target_pairs={{0,2},{1,3},{2,0},{3,1},{4,6},{5,7},{6,4},{7,5},{8,10},{9,11},{10,... | collective-permute-start | bytes 786440 | tf_op jit(solution)/shard_map/ppermute | solution.py:134
  38.2 9.4 %copy-start = (f32[8,256]{1,0:T(8,128)S(1)}, f32[8,256]{1,0:T(8,128)}, u32[]{:S(2)}) copy-start(f32[8,256]{1,0:T(8,128)} %rhs.1) | copy-start | bytes 24580
  45.2 4.3 %collective-permute-start.3 = (f32[1536,128]{1,0:T(8,128)S(1)}, f32[1536,128]{1,0:T(8,128)S(1)}, u32[]{:S(2)}, u32[]{:S(2)}) collective-permute-start(f32[1536,128]{1,0:T(8,128)S(1)} %pad_maximum_fusion), channel_id=1, source_target_pairs={{0,1},{1,0},{2,3},{3,2},{4,5},{5,4},{6,7},{7,6},{8,9},{9,8},{10,11... | collective-permute-start | bytes 2359304 | tf_op jit(solution)/shard_map/ppermute | solution.py:137
